TPU v7x, 32 devices: a whole 2x2x4 slice. The times are simulated.
32 devices in a mesh: rows: 16 (over z, y, x), probes: 2 (over core).
Axes of the slice: x: 2, y: 2, z: 4, core: 2. Of those that a mesh axis runs over, the one named last changes fastest.
Arguments:
- probes: bfloat16 [32, 16, 256], P('rows', 'probes'), parts along dimension 1, may hold values from -6 to 6
- factor: bfloat16 [32, 4, 256, 256], P('rows'), may hold values from -0.125 to 0.125
- inverses: bfloat16 [32, 256, 256], P('rows')
- pattern: int32 [32, 4], replicated, may hold values from -1 to 23, as said below
- owner: int32 [32], replicated, may hold values from 0 to 31, each once
Outputs:
- solution: bfloat16 [32, 16, 256], P('rows', 'probes'), parts along dimension 1
- selected: bfloat16 [32, 10, 256, 256], P('rows', 'probes'), parts along dimension 1
There are 2 independent parts, one for each index of `probes`. A program takes and returns all parts, laid end to end along the dimension named above; an argument that names none is the same for every part. Nothing has to cross between parts.
Inputs may be any that keep to these rules, and one draw needn't show every extreme that they name: `pattern`: Block-rows of the first level have only -1; every other block-row i names 4 different block-columns, all in levels below the level of i, one of them the block-row just before the first block-row of its own level.
All inputs are finite; a program needn't handle non-finite values.
Results may differ from a plain program's by a relative error of at most 0.012.
Values may be sent and summed in bfloat16 or wider, within the bound.
A program may use at most 64 MiB of HBM per device.

v0:
```python
import jax
import jax.numpy as jnp
from jax import lax
from jax.sharding import PartitionSpec as P

LEVELS = 4


def body(probes, factor, inverses, pattern, owner):
    f32 = jnp.float32
    bf16 = jnp.bfloat16
    me = lax.axis_index("rows")
    local = probes.shape[0]
    count = probes.shape[1]
    total = owner.shape[0]
    width = total // LEVELS
    iota = jnp.arange(total, dtype=jnp.int32)
    row_of_slot = jnp.sum(jnp.where(owner[None, :] == iota[:, None], iota[None, :], 0), axis=1)
    my_slots = me * local + jnp.arange(local, dtype=jnp.int32)
    my_rows = row_of_slot[my_slots]
    my_level = my_rows // width
    cols = pattern[my_rows]
    valid = cols >= 0
    source = owner[jnp.maximum(cols, 0)]
    picker = jnp.logical_and(source[:, :, None] == iota[None, None, :], valid[:, :, None])
    picker_half = picker.astype(bf16)
    picker_full = picker.astype(f32)
    all_probes = lax.all_gather(probes, "rows", axis=0, tiled=True)
    solved_all = jnp.zeros((total, count, probes.shape[2]), bf16)
    own_solved = jnp.zeros_like(probes)
    for level in range(LEVELS):
        near = jnp.einsum(
            "rkd,dpb->rkpb", picker_half, solved_all, preferred_element_type=f32
        ).astype(bf16)
        partial_value = jnp.einsum("rkpb,rkab->rpa", near, factor, preferred_element_type=f32)
        resid = (probes.astype(f32) - partial_value).astype(bf16)
        value = jnp.einsum("rpb,rab->rpa", resid, inverses, preferred_element_type=f32).astype(bf16)
        own_solved = jnp.where((my_level == level)[:, None, None], value, own_solved)
        if level < LEVELS - 1:
            solved_all = lax.all_gather(own_solved, "rows", axis=0, tiled=True)
    accum = jnp.zeros(probes.shape, f32)
    own_back = jnp.zeros_like(probes)
    for level in range(LEVELS - 1, -1, -1):
        start = (own_solved.astype(f32) - accum).astype(bf16)
        value = jnp.einsum("rpb,rba->rpa", start, inverses, preferred_element_type=f32).astype(bf16)
        active = my_level == level
        own_back = jnp.where(active[:, None, None], value, own_back)
        if level > 0:
            terms = jnp.einsum("rpa,rkab->rkpb", own_back, factor, preferred_element_type=f32)
            terms = terms * active.astype(f32)[:, None, None, None]
            outgoing = jnp.einsum(
                "rkd,rkpb->dpb", picker_full, terms, precision=lax.Precision.HIGHEST
            )
            arrived = lax.all_to_all(outgoing, "rows", split_axis=0, concat_axis=0, tiled=True)
            pieces = arrived.reshape((total // local, local) + arrived.shape[1:])
            accum = accum + jnp.sum(pieces, axis=0)
    near_probes = jnp.einsum(
        "rkd,dpb->rkpb", picker_half, all_probes, preferred_element_type=f32
    ).astype(bf16)
    off = jnp.einsum("rpa,rkpb->rkab", own_back, near_probes, preferred_element_type=f32)
    diag = jnp.einsum("rpa,rpb->rab", own_back, probes, preferred_element_type=f32)
    selected = (jnp.concatenate([off, diag[:, None]], axis=1) / count).astype(bf16)
    return (own_back, selected)


def solution(mesh):
    return jax.shard_map(
        body,
        mesh=mesh,
        in_specs=(
            P("rows", "probes", None),
            P("rows", None, None, None),
            P("rows", None, None),
            P(),
            P(),
        ),
        out_specs=(P("rows", "probes", None), P("rows", "probes", None, None)),
        check_vma=False,
    )
```

profile of v0, /device:TPU:0, one launch (start us, length us, event | category | flops | bytes accessed | tf_op | source)
XLA Modules:
  0.0 203.1 jit_solution(4655492516423288549)
XLA Ops:
  0.6 0.0 copy-start
  0.6 0.0 copy-start.1
  0.7 0.0 copy-start.2
  0.7 0.9 select_reduce_fusion
  1.6 0.6 gather_fusion
  2.2 0.8 copy.38
  3.0 0.6 gather_fusion.1
  3.6 0.1 reshape.131
  3.7 1.3 gather_fusion.2
  5.0 0.1 reshape.130
  5.1 0.1 fusion.55
  5.1 0.1 convolution_convert_fusion.4
  5.3 0.0 copy-done
  5.3 1.5 fusion.12
  6.7 43.1 %all_gather.12 = bf16[32,8,256]{2,1,0:T(8,128)(2,1)S(1)} all-gather(bf16[2,8,256]{2,1,0:T(8,128)(2,1)S(1)} %fusion.12), channel_id=1, replica_groups=mesh['rows'=16,'probes'=2] {'rows'}, dimensions={0}, use_global_device_ids=true | all-gather | bytes 139264 | tf_op jit(solution)/shard_map/all_gather | solution.py:40
  49.8 0.1 convolution_convert_fusion.3
  50.0 0.0 copy-done.1
  50.0 0.5 fusion.13
  50.5 36.1 %all_gather.13 = bf16[32,8,256]{2,1,0:T(8,128)(2,1)S(1)} all-gather(bf16[2,8,256]{2,1,0:T(8,128)(2,1)S(1)} %fusion.13), channel_id=1, replica_groups=mesh['rows'=16,'probes'=2] {'rows'}, dimensions={0}, use_global_device_ids=true | all-gather | bytes 139264 | tf_op jit(solution)/shard_map/all_gather | solution.py:40
  86.6 0.1 convolution_convert_fusion.2
  86.8 0.5 fusion.14
  87.3 38.5 %all_gather.14 = bf16[32,8,256]{2,1,0:T(8,128)(2,1)S(1)} all-gather(bf16[2,8,256]{2,1,0:T(8,128)(2,1)S(1)} %fusion.14), channel_id=1, replica_groups=mesh['rows'=16,'probes'=2] {'rows'}, dimensions={0}, use_global_device_ids=true | all-gather | bytes 139264 | tf_op jit(solution)/shard_map/all_gather | solution.py:40
  125.7 0.1 convolution_convert_fusion.1
  125.9 0.5 fusion.15
  126.4 0.2 fusion.16
  126.5 0.3 fusion.3
  126.8 0.4 convolution_bitcast_fusion.4
  127.2 0.2 copy.47
  127.3 11.9 %all_to_all.15 = f32[32,8,256]{2,1,0:T(8,128)S(1)} all-to-all(f32[32,8,256]{2,1,0:T(8,128)S(1)} %copy.47), channel_id=1, replica_groups=mesh['rows'=16,'probes'=2] {'rows'}, dimensions={0} | all-to-all | bytes 524288 | tf_op jit(solution)/shard_map/all_to_all | solution.py:54
  139.2 0.1 fusion.17
  139.4 0.2 fusion.2
  139.6 0.4 convolution_bitcast_fusion.3
  140.0 0.2 copy.51
  140.2 13.3 %all_to_all.16 = f32[32,8,256]{2,1,0:T(8,128)S(1)} all-to-all(f32[32,8,256]{2,1,0:T(8,128)S(1)} %copy.51), channel_id=1, replica_groups=mesh['rows'=16,'probes'=2] {'rows'}, dimensions={0} | all-to-all | bytes 524288 | tf_op jit(solution)/shard_map/all_to_all | solution.py:54
  153.5 0.1 fusion.18
  153.6 0.2 fusion.1
  153.9 0.4 convolution_bitcast_fusion.2
  154.2 0.9 copy.56
  155.1 3.5 %all-to-all-start.2 = ((f32[32,8,256]{2,1,0:T(8,128)}), f32[32,8,256]{2,1,0:T(8,128)S(1)}, u32[]{:S(2)}, u32[]{:S(2)}) async-start(f32[32,8,256]{2,1,0:T(8,128)} %copy.56), calls=%async_computation.2 | async-start | bytes 524288 | tf_op jit(solution)/shard_map/all_to_all | solution.py:54
  158.6 41.6 %all_gather.15 = bf16[32,8,256]{2,1,0:T(8,128)(2,1)S(1)} all-gather(bf16[2,8,256]{2,1,0:T(8,128)(2,1)S(1)} %copy-done.2), channel_id=1, replica_groups=mesh['rows'=16,'probes'=2] {'rows'}, dimensions={0}, use_global_device_ids=true | all-gather | bytes 139264 | tf_op jit(solution)/shard_map/all_gather | solution.py:28
  200.3 0.1 convolution_convert_fusion
  200.4 0.0 all-to-all-done.2
  200.5 0.1 fusion.19
  200.6 0.3 convolution_bitcast_fusion.1
  200.9 0.5 convolution_bitcast_fusion
  201.4 0.3 fusion
  201.7 0.0 copy-done.3
  201.7 1.4 copy.62
  (15 shorter events, 0.1 us)
Async XLA Ops:
  0.6 4.7 %copy-start = (bf16[2,4,256,256]{3,2,1,0:T(8,128)(2,1)S(1)}, bf16[2,4,256,256]{3,2,1,0:T(8,128)(2,1)}, u32[]{:S(2)}) copy-start(bf16[2,4,256,256]{3,2,1,0:T(8,128)(2,1)} %param.6) | copy-start | bytes 3145732
  0.6 49.3 %copy-start.1 = (bf16[2,256,256]{2,1,0:T(8,128)(2,1)S(1)}, bf16[2,256,256]{2,1,0:T(8,128)(2,1)}, u32[]{:S(2)}) copy-start(bf16[2,256,256]{2,1,0:T(8,128)(2,1)} %param.7) | copy-start | bytes 786436
  0.7 49.3 %copy-start.2 = (bf16[2,8,256]{2,1,0:T(8,128)(2,1)S(1)}, bf16[2,8,256]{2,1,0:T(8,128)(2,1)}, u32[]{:S(2)}) copy-start(bf16[2,8,256]{2,1,0:T(8,128)(2,1)} %param.5) | copy-start | bytes 24580
  155.1 45.3 %all-to-all-start.2 = ((f32[32,8,256]{2,1,0:T(8,128)}), f32[32,8,256]{2,1,0:T(8,128)S(1)}, u32[]{:S(2)}, u32[]{:S(2)}) async-start(f32[32,8,256]{2,1,0:T(8,128)} %copy.56), calls=%async_computation.2 | async-start | bytes 524288 | tf_op jit(solution)/shard_map/all_to_all | solution.py:54
  200.6 1.1 copy-start.3
where the time goes:
time: 204 us; the launch traced here: 203 us
  blocking collectives  184 us (90%)
  matrix products  6.83 us (3%)
  local copies, waits for them, and re-layouts  6.06 us (3%)
  starting transfers between devices  3.53 us (2%)
    all_gather x3, blocking collectives, body(): solved_all = lax.all_gather(own_solved, 'rows', axis=0, tiled=True)  118 us
    all_gather x1, blocking collectives, body(): all_probes = lax.all_gather(probes, 'rows', axis=0, tiled=True)  41.6 us
    all_to_all x2, blocking collectives, body(): lax.all_to_all(outgoing, 'rows', split_axis=0, concat_axis=0, tiled=True)  25.2 us
  transfers between devices with their start and end apart: 1, of which 0 were waited for; matrix products, arithmetic and copies ran while one was open for 0% of the time, Pallas kernels for 0%

commit v1 on v0

v1 whole, which is shorter than its diff:
```python
import functools

import jax
import jax.numpy as jnp
from jax import lax
from jax.experimental import pallas as pl
from jax.experimental.pallas import tpu as pltpu
from jax.sharding import PartitionSpec as P

LEVELS = 4
ROUNDS = LEVELS - 1
MESH = pl.DeviceIdType.MESH
F32 = jnp.float32
BF16 = jnp.bfloat16


def dot_nt(a, b):
    return lax.dot_general(a, b, (((1,), (1,)), ((), ())), preferred_element_type=F32)


def dot_nn(a, b):
    return lax.dot_general(a, b, (((1,), (0,)), ((), ())), preferred_element_type=F32)


def dot_tn(a, b):
    return lax.dot_general(a, b, (((0,), (0,)), ((), ())), preferred_element_type=F32)


def solve_kernel(n, local, count, neighbors, total, *refs):
    probes_ref, factor_hbm, inv_hbm, pattern_ref, owner_ref = refs[:5]
    back_ref, near_ref = refs[5:7]
    scratch = refs[7:]
    factor_ref, inv_ref, terms_ref, table_ref, all_probes = scratch[:5]
    ahead = scratch[5 : 5 + ROUNDS]
    outs = scratch[5 + ROUNDS : 5 + 2 * ROUNDS]
    arrive = scratch[5 + 2 * ROUNDS : 5 + 3 * ROUNDS]
    load_sem, send_sem, recv_sem = scratch[5 + 3 * ROUNDS :]
    me = lax.axis_index("rows")

    load_inv = pltpu.make_async_copy(inv_hbm, inv_ref, load_sem.at[0])
    load_factor = pltpu.make_async_copy(factor_hbm, factor_ref, load_sem.at[1])
    load_inv.start()
    load_factor.start()

    def peer(step):
        return lax.rem(me + step, n)

    barrier = pltpu.get_barrier_semaphore()

    def greet(step, carry):
        pl.semaphore_signal(barrier, inc=1, device_id={"rows": peer(step)}, device_id_type=MESH)
        return carry

    lax.fori_loop(1, n, greet, 0)

    def halves(block):
        wide = block.astype(F32)
        return [wide[r * count : (r + 1) * count] for r in range(local)]

    def pick(ref, slot, valid):
        parts = halves(ref[lax.div(slot, local)])
        at = lax.rem(slot, local)
        value = parts[0]
        for r in range(1, local):
            value = jnp.where(at == r, parts[r], value)
        return jnp.where(valid, value, jnp.zeros_like(value)).astype(BF16)

    def send(ref, step, at):
        to = peer(step)
        return pltpu.make_async_remote_copy(
            src_ref=ref[0].at[ref[1](to)],
            dst_ref=ref[2].at[me],
            send_sem=send_sem.at[at],
            recv_sem=recv_sem.at[at],
            device_id={"rows": to},
            device_id_type=MESH,
        )

    def whole_of(ref, at):
        every = ref.at[pl.ds(0, n - 1)]
        return pltpu.make_async_remote_copy(
            src_ref=every,
            dst_ref=every,
            send_sem=send_sem.at[at],
            recv_sem=recv_sem.at[at],
            device_id={"rows": peer(1)},
            device_id_type=MESH,
        )

    def broadcast(ref, at):
        def one(step, carry):
            send((ref, lambda to: me, ref), step, at).start()
            return carry

        lax.fori_loop(1, n, one, 0)

    probes = [probes_ref[r] for r in range(local)]
    probes_wide = [p.astype(F32) for p in probes]

    load_inv.wait()

    def solve_ahead(resid):
        return [dot_nt(resid[r], inv_ref[r]).astype(BF16) for r in range(local)]

    def store_rows(ref, at, values):
        ref[at] = jnp.concatenate([v.astype(F32) for v in values], axis=0).astype(BF16)

    solved = solve_ahead(probes)
    store_rows(ahead[0], me, solved)
    store_rows(all_probes, me, probes)

    pl.semaphore_wait(barrier, n - 1)
    broadcast(ahead[0], 0)
    broadcast(all_probes, 2 * ROUNDS)

    sources, valids = [], []
    for r in range(local):
        slot = me * local + r
        row = lax.fori_loop(
            0, total, lambda i, found: jnp.where(owner_ref[i] == slot, i, found), 0, unroll=8
        )
        cols = [pattern_ref[row, k] for k in range(neighbors)]
        valids.append([c >= 0 for c in cols])
        sources.append([owner_ref[jnp.maximum(c, 0)] for c in cols])

    def fill(slot, carry):
        for r in range(local):
            found = neighbors
            for k in range(neighbors):
                here = jnp.logical_and(sources[r][k] == slot, valids[r][k])
                found = jnp.where(here, k, found)
            table_ref[r, slot] = found
        return carry

    lax.fori_loop(0, total, fill, 0)
    for r in range(local):
        terms_ref[r, neighbors] = jnp.zeros((count, probes_wide[0].shape[1]), F32)

    load_factor.wait()

    for level in range(1, LEVELS):
        whole_of(ahead[level - 1], level - 1).wait_recv()
        resid = []
        for r in range(local):
            total_value = jnp.zeros_like(probes_wide[r])
            for k in range(neighbors):
                near = pick(ahead[level - 1], sources[r][k], valids[r][k])
                total_value += dot_nt(near, factor_ref[r, k])
            resid.append((probes_wide[r] - total_value).astype(BF16))
        solved = solve_ahead(resid)
        if level < ROUNDS:
            store_rows(ahead[level], me, solved)
            broadcast(ahead[level], level)

    solved_wide = [v.astype(F32) for v in solved]
    start = solved
    for turn in range(LEVELS):
        backed = [dot_nn(start[r], inv_ref[r]).astype(BF16) for r in range(local)]
        if turn == ROUNDS:
            break
        for r in range(local):
            for k in range(neighbors):
                terms_ref[r, k] = dot_nn(backed[r], factor_ref[r, k])

        def part(device):
            rows = []
            for q in range(local):
                slot = device * local + q
                value = terms_ref[0, table_ref[0, slot]]
                for r in range(1, local):
                    value += terms_ref[r, table_ref[r, slot]]
                rows.append(value)
            return jnp.concatenate(rows, axis=0).astype(BF16)

        out, into, at = outs[turn], arrive[turn], ROUNDS + turn

        def one(step, carry):
            to = peer(step)
            out[to] = part(to)
            send((out, lambda d: d, into), step, at).start()
            return carry

        lax.fori_loop(1, n, one, 0)
        into[me] = part(me)
        whole_of(into, at).wait_recv()
        acc = lax.fori_loop(
            1, n, lambda d, sum_: sum_ + into[d].astype(F32), into[0].astype(F32), unroll=True
        )
        start = [
            (solved_wide[r] - acc[r * count : (r + 1) * count]).astype(BF16) for r in range(local)
        ]

    whole_of(all_probes, 2 * ROUNDS).wait_recv()
    for r in range(local):
        back_ref[r] = backed[r]
        width = probes_wide[r].shape[1]
        for k in range(neighbors):
            near_ref[r, :, k * width : (k + 1) * width] = pick(
                all_probes, sources[r][k], valids[r][k]
            )
        near_ref[r, :, neighbors * width :] = probes[r]

    for level in range(ROUNDS):
        whole_of(ahead[level], level).wait_send()
        whole_of(outs[level], ROUNDS + level).wait_send()
    whole_of(all_probes, 2 * ROUNDS).wait_send()


def select_kernel(local, count, blocks, back_ref, near_ref, sol_ref, sel_hbm, sel_ref, sems):
    copies = []
    width = back_ref.shape[2]
    for r in range(local):
        value = back_ref[r]
        sol_ref[r] = value
        near = near_ref[r]
        for k in range(blocks):
            product = dot_tn(value, near[:, k * width : (k + 1) * width])
            sel_ref[r, k] = (product / count).astype(BF16)
        copy = pltpu.make_async_copy(sel_ref.at[r], sel_hbm.at[r], sems.at[r])
        copy.start()
        copies.append(copy)
    for copy in copies:
        copy.wait()


def solution(mesh):
    n = mesh.shape["rows"]

    def body(probes, factor, inverses, pattern, owner):
        local, count, width = probes.shape
        neighbors = factor.shape[1]
        total = owner.shape[0]
        rows = local * count
        vmem = pl.BlockSpec(memory_space=pltpu.VMEM)
        smem = pl.BlockSpec(memory_space=pltpu.SMEM)
        anywhere = pl.BlockSpec(memory_space=pl.ANY)
        gathered = pltpu.VMEM((n, rows, width), BF16)
        backed, near = pl.pallas_call(
            functools.partial(solve_kernel, n, local, count, neighbors, total),
            out_shape=(
                jax.ShapeDtypeStruct((local, count, width), BF16),
                jax.ShapeDtypeStruct((local, count, (neighbors + 1) * width), BF16),
            ),
            in_specs=[vmem, anywhere, anywhere, smem, smem],
            out_specs=(vmem, vmem),
            scratch_shapes=[
                pltpu.VMEM(factor.shape, BF16),
                pltpu.VMEM(inverses.shape, BF16),
                pltpu.VMEM((local, neighbors + 1, count, width), F32),
                pltpu.SMEM((local, total), jnp.int32),
                gathered,
            ]
            + [gathered] * (3 * ROUNDS)
            + [
                pltpu.SemaphoreType.DMA((2,)),
                pltpu.SemaphoreType.DMA((2 * ROUNDS + 1,)),
                pltpu.SemaphoreType.DMA((2 * ROUNDS + 1,)),
            ],
            compiler_params=pltpu.CompilerParams(
                collective_id=0, has_side_effects=True, vmem_limit_bytes=40 * 1024 * 1024
            ),
            name="solve_rounds",
        )(probes, factor, inverses, pattern, owner)
        sol, selected = pl.pallas_call(
            functools.partial(select_kernel, local, count, neighbors + 1),
            out_shape=(
                jax.ShapeDtypeStruct((local, count, width), BF16),
                jax.ShapeDtypeStruct((local, neighbors + 1, width, width), BF16),
            ),
            in_specs=[vmem, vmem],
            out_specs=(vmem, anywhere),
            scratch_shapes=[
                pltpu.VMEM((local, neighbors + 1, width, width), BF16),
                pltpu.SemaphoreType.DMA((local,)),
            ],
            compiler_params=pltpu.CompilerParams(vmem_limit_bytes=16 * 1024 * 1024),
            name="select_blocks",
        )(backed, near)
        return sol, selected

    return jax.shard_map(
        body,
        mesh=mesh,
        in_specs=(
            P("rows", "probes", None),
            P("rows", None, None, None),
            P("rows", None, None),
            P(),
            P(),
        ),
        out_specs=(P("rows", "probes", None), P("rows", "probes", None, None)),
        check_vma=False,
    )
```

time: 204 us -> 50.1 us (0.25)
  blocking collectives: 184 us -> 0 us
  Pallas kernels: 0 us -> 44.9 us
  matrix products: 6.83 us -> 0 us
  starting transfers between devices: 3.53 us -> 0 us
    all_gather x4 -> x0, blocking collectives: 159 us -> none  [the longest x3 118 us: body(): solved_all = lax.all_gather(own_solved, 'rows', axis=0, tiled=True)]
    pallas_call x0 -> x2, Pallas kernels: none -> 44.9 us  [the longest x1 42.8 us: body(): pl.pallas_call(functools.partial(solve_kernel, n, local, count, neighbors...]
    all_to_all x2 -> x0, blocking collectives: 25.2 us -> none  [body(): lax.all_to_all(outgoing, 'rows', split_axis=0, concat_axis=0, tiled=True)]
    dot_general x21 -> x0, matrix products: 6.83 us -> none  [the longest x4 2.91 us: body(): jnp.einsum('rpb,rab->rpa', resid, inverses, preferred_element_type=f32)]
    all_to_all x1 -> x0, starting transfers between devices: 3.53 us -> none  [body(): lax.all_to_all(outgoing, 'rows', split_axis=0, concat_axis=0, tiled=True)]
    gather x4 -> x0, local copies, waits for them, and re-layouts: 2.57 us -> none  [the longest x2 1.38 us: body(): source = owner[jnp.maximum(cols, 0)]]
    unnamed x10 -> x9, local copies, waits for them, and re-layouts: 2.23 us -> 4.29 us
  transfers between devices with their start and end apart: 1 -> 0, of which waited for: 0 -> 0; matrix products, arithmetic and copies ran while one was open for 0% -> 0% of each run, Pallas kernels for 0% -> 0%
where the time goes in v1:
time: 50.1 us; the launch traced here: 49.8 us
  Pallas kernels  44.9 us (90%)
  local copies, waits for them, and re-layouts  4.29 us (9%)
  between operations  0.64 us (1%)
    pallas_call x1, Pallas kernels, body(): pl.pallas_call(functools.partial(solve_kernel, n, local, count, neighbors...  42.8 us
    unnamed x9, local copies, waits for them, and re-layouts  4.29 us
    pallas_call x1, Pallas kernels, body(): pl.pallas_call(functools.partial(select_kernel, local, count, neighbors +...  2.06 us

profile of v1, /device:TPU:0, one launch (start us, length us, event | category | flops | bytes accessed | tf_op | source)
XLA Modules:
  0.0 49.8 jit_solution(8583245029441674658)
XLA Ops:
  0.6 0.8 %copy.7.refs_3_ = s32[32,4]{1,0:T(8,128)S(1)} copy(s32[32,4]{0,1:T(4,128)} %param.8) | data formatting | bytes 1024 | tf_op args[3]
  1.4 0.0 copy-start
  1.4 1.2 %copy-done = bf16[2,4,256,256]{3,2,1,0:T(8,128)(2,1)S(1)} copy-done((bf16[2,4,256,256]{3,2,1,0:T(8,128)(2,1)S(1)}, bf16[2,4,256,256]{3,2,1,0:T(8,128)(2,1)}, u32[]{:S(2)}) %copy-start) | copy-done | bytes 1048600
  2.6 0.0 copy-start.1
  2.6 0.9 %copy-done.1 = bf16[2,256,256]{2,1,0:T(8,128)(2,1)S(1)} copy-done((bf16[2,256,256]{2,1,0:T(8,128)(2,1)S(1)}, bf16[2,256,256]{2,1,0:T(8,128)(2,1)}, u32[]{:S(2)}) %copy-start.1) | copy-done | bytes 262168
  3.6 0.0 copy-start.2
  3.6 0.7 %copy-done.2 = bf16[2,8,256]{2,1,0:T(8,128)(2,1)S(1)} copy-done((bf16[2,8,256]{2,1,0:T(8,128)(2,1)S(1)}, bf16[2,8,256]{2,1,0:T(8,128)(2,1)}, u32[]{:S(2)}) %copy-start.2) | copy-done | bytes 8216
  4.3 0.0 copy-start.3
  4.3 0.7 %copy-done.3 = s32[32]{0:T(128)S(1)} copy-done((s32[32]{0:T(128)S(1)}, s32[32]{0:T(128)}, u32[]{:S(2)}) %copy-start.3) | copy-done | bytes 152
  4.9 42.8 %solve_rounds.1 = (bf16[2,8,256]{2,1,0:T(8,128)(2,1)S(1)}, bf16[2,8,1280]{2,1,0:T(8,128)(2,1)S(1)}) custom-call(bf16[2,8,256]{2,1,0:T(8,128)(2,1)S(1)} %copy-done.2, bf16[2,4,256,256]{3,2,1,0:T(8,128)(2,1)S(1)} %copy-done, bf16[2,256,256]{2,1,0:T(8,128)(2,1)S(1)} %copy-done.1, s32[32,4]{1,0:T(8,128)S(1)} %copy.7.refs_3_, s32[32]{0:T(128)S(1)} %copy-done.3), custom_call_target="tpu_custom_call" | custom-call | tf_op jit(solution)/shard_map/solve_rounds/pallas_call | solution.py:238
  47.8 2.1 %select_blocks.1 = (bf16[2,8,256]{2,1,0:T(8,128)(2,1)}, bf16[2,5,256,256]{3,2,1,0:T(8,128)(2,1)}) custom-call(bf16[2,8,256]{2,1,0:T(8,128)(2,1)S(1)} %get-tuple-element.4.back_ref, bf16[2,8,1280]{2,1,0:T(8,128)(2,1)S(1)} %get-tuple-element.5.near_ref), custom_call_target="tpu_custom_call" | custom-call | tf_op jit(solution)/shard_map/select_blocks/pallas_call | solution.py:264
Async XLA Ops:
  1.4 1.2 %copy-start = (bf16[2,4,256,256]{3,2,1,0:T(8,128)(2,1)S(1)}, bf16[2,4,256,256]{3,2,1,0:T(8,128)(2,1)}, u32[]{:S(2)}) copy-start(bf16[2,4,256,256]{3,2,1,0:T(8,128)(2,1)} %refs_1_.1) | copy-start | bytes 3145732
  2.6 0.9 %copy-start.1 = (bf16[2,256,256]{2,1,0:T(8,128)(2,1)S(1)}, bf16[2,256,256]{2,1,0:T(8,128)(2,1)}, u32[]{:S(2)}) copy-start(bf16[2,256,256]{2,1,0:T(8,128)(2,1)} %refs_2_.1) | copy-start | bytes 786436
  3.6 0.7 %copy-start.2 = (bf16[2,8,256]{2,1,0:T(8,128)(2,1)S(1)}, bf16[2,8,256]{2,1,0:T(8,128)(2,1)}, u32[]{:S(2)}) copy-start(bf16[2,8,256]{2,1,0:T(8,128)(2,1)} %refs_0_.1) | copy-start | bytes 24580
  4.3 0.7 %copy-start.3 = (s32[32]{0:T(128)S(1)}, s32[32]{0:T(128)}, u32[]{:S(2)}) copy-start(s32[32]{0:T(128)} %refs_4_.1) | copy-start | bytes 388

commit v2 on v1

--- a/solution.py
+++ b/solution.py
@@ -30,11 +30,13 @@
     probes_ref, factor_hbm, inv_hbm, pattern_ref, owner_ref = refs[:5]
     back_ref, near_ref = refs[5:7]
     scratch = refs[7:]
-    factor_ref, inv_ref, terms_ref, table_ref, all_probes = scratch[:5]
-    ahead = scratch[5 : 5 + ROUNDS]
-    outs = scratch[5 + ROUNDS : 5 + 2 * ROUNDS]
-    arrive = scratch[5 + 2 * ROUNDS : 5 + 3 * ROUNDS]
-    load_sem, send_sem, recv_sem = scratch[5 + 3 * ROUNDS :]
+    factor_ref, inv_ref, factor_t, inv_t, terms_ref, table_ref, all_probes = scratch[:7]
+    ahead = scratch[7 : 7 + ROUNDS]
+    outs = scratch[7 + ROUNDS : 7 + 2 * ROUNDS]
+    arrive = scratch[7 + 2 * ROUNDS : 7 + 3 * ROUNDS]
+    load_sem, send_sem, recv_sem = scratch[7 + 3 * ROUNDS :]
+    unroll = n <= 16
+    group = max(g for g in range(1, 6) if (n - 1) % g == 0)
     me = lax.axis_index("rows")
 
     load_inv = pltpu.make_async_copy(inv_hbm, inv_ref, load_sem.at[0])
@@ -43,7 +45,9 @@
     load_factor.start()
 
     def peer(step):
-        return lax.rem(me + step, n)
+        odd = step % 2
+        away = n // 2 + odd * ((step + 1) // 2) - (1 - odd) * (step // 2)
+        return lax.rem(me + away, n)
 
     barrier = pltpu.get_barrier_semaphore()
 
@@ -51,7 +55,7 @@
         pl.semaphore_signal(barrier, inc=1, device_id={"rows": peer(step)}, device_id_type=MESH)
         return carry
 
-    lax.fori_loop(1, n, greet, 0)
+    lax.fori_loop(0, n - 1, greet, 0, unroll=unroll)
 
     def halves(block):
         wide = block.astype(F32)
@@ -83,35 +87,39 @@
             dst_ref=every,
             send_sem=send_sem.at[at],
             recv_sem=recv_sem.at[at],
-            device_id={"rows": peer(1)},
+            device_id={"rows": peer(0)},
             device_id_type=MESH,
         )
 
-    def broadcast(ref, at):
+    def broadcast(ref, at, first=0, last=n - 1):
         def one(step, carry):
             send((ref, lambda to: me, ref), step, at).start()
             return carry
 
-        lax.fori_loop(1, n, one, 0)
+        lax.fori_loop(first, last, one, 0, unroll=unroll)
+
+    def share_probes(turn):
+        pieces = 2 * ROUNDS - 1
+        size = -(-(n - 1) // pieces)
+        first = min(turn * size, n - 1)
+        last = min(first + size, n - 1)
+        if last > first:
+            broadcast(all_probes, 2 * ROUNDS, first, last)
 
     probes = [probes_ref[r] for r in range(local)]
     probes_wide = [p.astype(F32) for p in probes]
 
     load_inv.wait()
 
-    def solve_ahead(resid):
-        return [dot_nt(resid[r], inv_ref[r]).astype(BF16) for r in range(local)]
-
     def store_rows(ref, at, values):
         ref[at] = jnp.concatenate([v.astype(F32) for v in values], axis=0).astype(BF16)
 
-    solved = solve_ahead(probes)
+    solved = [dot_nt(probes[r], inv_ref[r]).astype(BF16) for r in range(local)]
     store_rows(ahead[0], me, solved)
     store_rows(all_probes, me, probes)
 
     pl.semaphore_wait(barrier, n - 1)
     broadcast(ahead[0], 0)
-    broadcast(all_probes, 2 * ROUNDS)
 
     sources, valids = [], []
     for r in range(local):
@@ -119,7 +127,7 @@
         row = lax.fori_loop(
             0, total, lambda i, found: jnp.where(owner_ref[i] == slot, i, found), 0, unroll=8
         )
-        cols = [pattern_ref[row, k] for k in range(neighbors)]
+        cols = [pattern_ref[k, row] for k in range(neighbors)]
         valids.append([c >= 0 for c in cols])
         sources.append([owner_ref[jnp.maximum(c, 0)] for c in cols])
 
@@ -132,22 +140,27 @@
             table_ref[r, slot] = found
         return carry
 
-    lax.fori_loop(0, total, fill, 0)
+    lax.fori_loop(0, total, fill, 0, unroll=4)
     for r in range(local):
         terms_ref[r, neighbors] = jnp.zeros((count, probes_wide[0].shape[1]), F32)
 
     load_factor.wait()
+    for r in range(local):
+        inv_t[r] = inv_ref[r].T
+        for k in range(neighbors):
+            factor_t[r, k] = factor_ref[r, k].T
 
     for level in range(1, LEVELS):
         whole_of(ahead[level - 1], level - 1).wait_recv()
+        share_probes(level - 1)
         resid = []
         for r in range(local):
             total_value = jnp.zeros_like(probes_wide[r])
             for k in range(neighbors):
                 near = pick(ahead[level - 1], sources[r][k], valids[r][k])
-                total_value += dot_nt(near, factor_ref[r, k])
+                total_value += dot_nn(near, factor_t[r, k])
             resid.append((probes_wide[r] - total_value).astype(BF16))
-        solved = solve_ahead(resid)
+        solved = [dot_nn(resid[r], inv_t[r]).astype(BF16) for r in range(local)]
         if level < ROUNDS:
             store_rows(ahead[level], me, solved)
             broadcast(ahead[level], level)
@@ -174,15 +187,20 @@
 
         out, into, at = outs[turn], arrive[turn], ROUNDS + turn
 
-        def one(step, carry):
-            to = peer(step)
-            out[to] = part(to)
-            send((out, lambda d: d, into), step, at).start()
+        def some(chunk, carry):
+            steps = [chunk * group + i for i in range(group)]
+            values = [part(peer(step)) for step in steps]
+            for step, value in zip(steps, values):
+                out[peer(step)] = value
+            for step in steps:
+                send((out, lambda d: d, into), step, at).start()
             return carry
 
-        lax.fori_loop(1, n, one, 0)
+        lax.fori_loop(0, (n - 1) // group, some, 0, unroll=unroll)
         into[me] = part(me)
         whole_of(into, at).wait_recv()
+        if turn < ROUNDS - 1:
+            share_probes(ROUNDS + turn)
         acc = lax.fori_loop(
             1, n, lambda d, sum_: sum_ + into[d].astype(F32), into[0].astype(F32), unroll=True
         )
@@ -246,6 +264,8 @@
             scratch_shapes=[
                 pltpu.VMEM(factor.shape, BF16),
                 pltpu.VMEM(inverses.shape, BF16),
+                pltpu.VMEM(factor.shape, BF16),
+                pltpu.VMEM(inverses.shape, BF16),
                 pltpu.VMEM((local, neighbors + 1, count, width), F32),
                 pltpu.SMEM((local, total), jnp.int32),
                 gathered,
@@ -257,10 +277,10 @@
                 pltpu.SemaphoreType.DMA((2 * ROUNDS + 1,)),
             ],
             compiler_params=pltpu.CompilerParams(
-                collective_id=0, has_side_effects=True, vmem_limit_bytes=40 * 1024 * 1024
+                collective_id=0, has_side_effects=True, vmem_limit_bytes=60 * 1024 * 1024
             ),
             name="solve_rounds",
-        )(probes, factor, inverses, pattern, owner)
+        )(probes, factor, inverses, pattern.T, owner)
         sol, selected = pl.pallas_call(
             functools.partial(select_kernel, local, count, neighbors + 1),
             out_shape=(
@@ -273,7 +293,7 @@
                 pltpu.VMEM((local, neighbors + 1, width, width), BF16),
                 pltpu.SemaphoreType.DMA((local,)),
             ],
-            compiler_params=pltpu.CompilerParams(vmem_limit_bytes=16 * 1024 * 1024),
+            compiler_params=pltpu.CompilerParams(vmem_limit_bytes=60 * 1024 * 1024),
             name="select_blocks",
         )(backed, near)
         return sol, selected

time: 50.1 us -> 48.6 us (0.970)
  local copies, waits for them, and re-layouts: 4.29 us -> 0 us
  Pallas kernels: 44.9 us -> 47.7 us
    unnamed x9 -> x0, local copies, waits for them, and re-layouts: 4.29 us -> none
    pallas_call x1, Pallas kernels: 42.8 us -> 44.8 us  [body(): pl.pallas_call(functools.partial(solve_kernel, n, local, count, neighbors...]
    pallas_call x1, Pallas kernels: 2.06 us -> 2.85 us  [body(): pl.pallas_call(functools.partial(select_kernel, local, count, neighbors +...]
where the time goes in v2:
time: 48.6 us; the launch traced here: 48.3 us
  Pallas kernels  47.7 us (98%)
  between operations  0.64 us (1%)
    pallas_call x1, Pallas kernels, body(): pl.pallas_call(functools.partial(solve_kernel, n, local, count, neighbors...  44.8 us
    pallas_call x1, Pallas kernels, body(): pl.pallas_call(functools.partial(select_kernel, local, count, neighbors +...  2.85 us

profile of v2, /device:TPU:0, one launch (start us, length us, event | category | flops | bytes accessed | tf_op | source)
XLA Modules:
  0.0 48.3 jit_solution(4825785730117374315)
XLA Ops:
  0.6 44.8 %solve_rounds.1 = (bf16[2,8,256]{2,1,0:T(8,128)(2,1)}, bf16[2,8,1280]{2,1,0:T(8,128)(2,1)}) custom-call(bf16[2,8,256]{2,1,0:T(8,128)(2,1)} %refs_0_.1, bf16[2,4,256,256]{3,2,1,0:T(8,128)(2,1)} %refs_1_.1, bf16[2,256,256]{2,1,0:T(8,128)(2,1)} %refs_2_.1, s32[4,32]{1,0:T(4,128)} %bitcast.1, s32[32]{0:T(128)} %refs_4_.1), custom_call_target="tpu_custom_call" | custom-call | tf_op jit(solution)/shard_map/solve_rounds/pallas_call | solution.py:256
  45.5 2.9 %select_blocks.1 = (bf16[2,8,256]{2,1,0:T(8,128)(2,1)}, bf16[2,5,256,256]{3,2,1,0:T(8,128)(2,1)}) custom-call(bf16[2,8,256]{2,1,0:T(8,128)(2,1)} %get-tuple-element.4.back_ref, bf16[2,8,1280]{2,1,0:T(8,128)(2,1)} %get-tuple-element.5.near_ref), custom_call_target="tpu_custom_call" | custom-call | tf_op jit(solution)/shard_map/select_blocks/pallas_call | solution.py:284

commit v3 on v2

v3 whole, which is shorter than its diff:
```python
import functools

import jax
import jax.numpy as jnp
from jax import lax
from jax.experimental import pallas as pl
from jax.experimental.pallas import tpu as pltpu
from jax.sharding import PartitionSpec as P

LEVELS = 4
ROUNDS = LEVELS - 1
MESH = pl.DeviceIdType.MESH
F32 = jnp.float32
BF16 = jnp.bfloat16


def dot_nt(a, b):
    return lax.dot_general(a, b, (((1,), (1,)), ((), ())), preferred_element_type=F32)


def dot_nn(a, b):
    return lax.dot_general(a, b, (((1,), (0,)), ((), ())), preferred_element_type=F32)


def dot_tn(a, b):
    return lax.dot_general(a, b, (((0,), (0,)), ((), ())), preferred_element_type=F32)


def solve_kernel(n, inner, local, count, neighbors, total, *refs):
    outer = n // inner
    probes_ref, factor_hbm, inv_hbm, pattern_ref, owner_ref = refs[:5]
    back_ref, near_ref = refs[5:7]
    scratch = refs[7:]
    factor_ref, inv_ref, factor_t, inv_t, terms_ref, table_ref, all_probes = scratch[:7]
    ahead = scratch[7 : 7 + ROUNDS]
    outs = scratch[7 + ROUNDS : 7 + 2 * ROUNDS]
    arrive = scratch[7 + 2 * ROUNDS : 7 + 3 * ROUNDS]
    mids = scratch[7 + 3 * ROUNDS : 7 + 4 * ROUNDS]
    finals = scratch[7 + 4 * ROUNDS : 7 + 5 * ROUNDS]
    load_sem, send_sem, recv_sem = scratch[7 + 5 * ROUNDS :]
    unroll = n <= 16
    me = lax.axis_index("rows")
    high = me // inner
    low = me % inner

    load_inv = pltpu.make_async_copy(inv_hbm, inv_ref, load_sem.at[0])
    load_factor = pltpu.make_async_copy(factor_hbm, factor_ref, load_sem.at[1])
    load_inv.start()
    load_factor.start()

    def far(step):
        return lax.rem(high + step, outer)

    def near(step):
        return lax.rem(low + step, inner)

    def copy_to(to, src, dst, at):
        return pltpu.make_async_remote_copy(
            src_ref=src,
            dst_ref=dst,
            send_sem=send_sem.at[at],
            recv_sem=recv_sem.at[at],
            device_id={"rows": to},
            device_id_type=MESH,
        )

    def far_copy(step, src, dst, at):
        return copy_to(far(step) * inner + low, src, dst, at)

    def near_copy(step, src, dst, at):
        return copy_to(high * inner + near(step), src, dst, at)

    def each(steps, one):
        def body(step, carry):
            one(step)
            return carry

        lax.fori_loop(1, steps, body, 0, unroll=unroll)

    barrier = pltpu.get_barrier_semaphore()

    def greet(to):
        pl.semaphore_signal(barrier, inc=1, device_id={"rows": to}, device_id_type=MESH)

    each(outer, lambda step: greet(far(step) * inner + low))
    each(inner, lambda step: greet(high * inner + near(step)))

    def halves(block):
        wide = block.astype(F32)
        return [wide[r * count : (r + 1) * count] for r in range(local)]

    def pick(ref, place, valid):
        parts = halves(ref[place[0], place[1]])
        value = parts[0]
        for r in range(1, local):
            value = jnp.where(place[2] == r, parts[r], value)
        return jnp.where(valid, value, jnp.zeros_like(value)).astype(BF16)

    def all_far(ref, at):
        every = ref.at[0, pl.ds(0, outer - 1)]
        return far_copy(1, every, every, at)

    def all_far_flat(ref, at):
        every = ref.at[pl.ds(0, outer - 1)]
        return far_copy(1, every, every, at)

    def all_near(ref, at):
        every = ref.at[pl.ds(0, inner - 1)]
        return near_copy(1, every, every, at)

    def gather_far(ref, at):
        own = ref.at[low, high]
        each(outer, lambda step: far_copy(step, own, own, at).start())

    def gather_near(ref, at):
        own = ref.at[low]
        each(inner, lambda step: near_copy(step, own, own, at).start())

    probes = [probes_ref[r] for r in range(local)]
    probes_wide = [p.astype(F32) for p in probes]

    load_inv.wait()

    def store_own(ref, values):
        ref[low, high] = jnp.concatenate([v.astype(F32) for v in values], axis=0).astype(BF16)

    solved = [dot_nt(probes[r], inv_ref[r]).astype(BF16) for r in range(local)]
    store_own(ahead[0], solved)
    store_own(all_probes, probes)

    pl.semaphore_wait(barrier, outer + inner - 2)
    gather_far(ahead[0], 0)

    sources, places, valids = [], [], []
    for r in range(local):
        slot = me * local + r
        row = lax.fori_loop(
            0, total, lambda i, found: jnp.where(owner_ref[i] == slot, i, found), 0, unroll=8
        )
        cols = [pattern_ref[k, row] for k in range(neighbors)]
        valids.append([c >= 0 for c in cols])
        slots = [owner_ref[jnp.maximum(c, 0)] for c in cols]
        sources.append(slots)
        places.append(
            [
                (
                    lax.rem(lax.div(s, local), inner),
                    lax.div(s, local * inner),
                    lax.rem(s, local),
                )
                for s in slots
            ]
        )

    all_far(ahead[0], 0).wait_recv()
    gather_near(ahead[0], 1)
    gather_far(all_probes, 4 * ROUNDS)

    def fill(slot, carry):
        for r in range(local):
            found = neighbors
            for k in range(neighbors):
                here = jnp.logical_and(sources[r][k] == slot, valids[r][k])
                found = jnp.where(here, k, found)
            table_ref[r, slot] = found
        return carry

    load_factor.wait()
    for r in range(local):
        for k in range(neighbors):
            factor_t[r, k] = factor_ref[r, k].T

    for level in range(1, LEVELS):
        last = ahead[level - 1]
        if level > 1:
            all_far(last, 2 * level - 2).wait_recv()
            gather_near(last, 2 * level - 1)
        all_near(last, 2 * level - 1).wait_recv()
        resid = []
        for r in range(local):
            total_value = jnp.zeros_like(probes_wide[r])
            for k in range(neighbors):
                value = pick(last, places[r][k], valids[r][k])
                total_value += dot_nn(value, factor_t[r, k])
            resid.append((probes_wide[r] - total_value).astype(BF16))
        solved = [dot_nt(resid[r], inv_ref[r]).astype(BF16) for r in range(local)]
        if level < ROUNDS:
            store_own(ahead[level], solved)
            gather_far(ahead[level], 2 * level)
        if level == 1:
            lax.fori_loop(0, total, fill, 0, unroll=4)
            for r in range(local):
                terms_ref[r, neighbors] = jnp.zeros((count, probes_wide[0].shape[1]), F32)
            all_far(all_probes, 4 * ROUNDS).wait_recv()
            gather_near(all_probes, 4 * ROUNDS + 1)

    solved_wide = [v.astype(F32) for v in solved]
    start = solved
    for turn in range(LEVELS):
        backed = [dot_nn(start[r], inv_ref[r]).astype(BF16) for r in range(local)]
        if turn == ROUNDS:
            break
        for r in range(local):
            for k in range(neighbors):
                terms_ref[r, k] = dot_nn(backed[r], factor_ref[r, k])

        def part(device):
            rows = []
            for q in range(local):
                slot = device * local + q
                value = terms_ref[0, table_ref[0, slot]]
                for r in range(1, local):
                    value += terms_ref[r, table_ref[r, slot]]
                rows.append(value)
            return jnp.concatenate(rows, axis=0)

        out, into, mid, final = outs[turn], arrive[turn], mids[turn], finals[turn]
        at = 2 * (ROUNDS + turn)

        def give(step):
            to = near(step)
            values = [part(z * inner + to).astype(BF16) for z in range(outer)]
            for z in range(outer):
                out[to, z] = values[z]
            near_copy(step, out.at[to], into.at[low], at).start()

        each(inner, give)
        own = [part(z * inner + low) for z in range(outer)]
        for z in range(outer):
            into[low, z] = own[z].astype(BF16)
        all_near(into, at).wait_recv()
        for z in range(outer):
            value = into[0, z].astype(F32)
            for p in range(1, inner):
                value += into[p, z].astype(F32)
            mid[z] = value.astype(BF16)
        each(
            outer,
            lambda step: far_copy(step, mid.at[far(step)], final.at[high], at + 1).start(),
        )
        final[high] = mid[high]
        all_far_flat(final, at + 1).wait_recv()
        acc = final[0].astype(F32)
        for z in range(1, outer):
            acc += final[z].astype(F32)
        start = [
            (solved_wide[r] - acc[r * count : (r + 1) * count]).astype(BF16) for r in range(local)
        ]

    all_near(all_probes, 4 * ROUNDS + 1).wait_recv()
    for r in range(local):
        back_ref[r] = backed[r]
        width = probes_wide[r].shape[1]
        for k in range(neighbors):
            near_ref[r, :, k * width : (k + 1) * width] = pick(
                all_probes, places[r][k], valids[r][k]
            )
        near_ref[r, :, neighbors * width :] = probes[r]

    for level in range(ROUNDS):
        all_far(ahead[level], 2 * level).wait_send()
        all_near(ahead[level], 2 * level + 1).wait_send()
        all_near(outs[level], 2 * (ROUNDS + level)).wait_send()
        all_far_flat(mids[level], 2 * (ROUNDS + level) + 1).wait_send()
    all_far(all_probes, 4 * ROUNDS).wait_send()
    all_near(all_probes, 4 * ROUNDS + 1).wait_send()


def select_kernel(local, count, blocks, back_ref, near_ref, sol_ref, sel_hbm, sel_ref, sems):
    copies = []
    width = back_ref.shape[2]
    for r in range(local):
        value = back_ref[r]
        sol_ref[r] = value
        near = near_ref[r]
        for k in range(blocks):
            product = dot_tn(value, near[:, k * width : (k + 1) * width])
            sel_ref[r, k] = (product / count).astype(BF16)
        copy = pltpu.make_async_copy(sel_ref.at[r], sel_hbm.at[r], sems.at[r])
        copy.start()
        copies.append(copy)
    for copy in copies:
        copy.wait()


def solution(mesh):
    n = mesh.shape["rows"]
    inner = max(d for d in range(1, n + 1) if n % d == 0 and d * d <= n)
    outer = n // inner

    def body(probes, factor, inverses, pattern, owner):
        local, count, width = probes.shape
        neighbors = factor.shape[1]
        total = owner.shape[0]
        rows = local * count
        vmem = pl.BlockSpec(memory_space=pltpu.VMEM)
        smem = pl.BlockSpec(memory_space=pltpu.SMEM)
        anywhere = pl.BlockSpec(memory_space=pl.ANY)
        gathered = pltpu.VMEM((inner, outer, rows, width), BF16)
        column = pltpu.VMEM((outer, rows, width), BF16)
        backed, near = pl.pallas_call(
            functools.partial(solve_kernel, n, inner, local, count, neighbors, total),
            out_shape=(
                jax.ShapeDtypeStruct((local, count, width), BF16),
                jax.ShapeDtypeStruct((local, count, (neighbors + 1) * width), BF16),
            ),
            in_specs=[vmem, anywhere, anywhere, smem, smem],
            out_specs=(vmem, vmem),
            scratch_shapes=[
                pltpu.VMEM(factor.shape, BF16),
                pltpu.VMEM(inverses.shape, BF16),
                pltpu.VMEM(factor.shape, BF16),
                pltpu.VMEM(inverses.shape, BF16),
                pltpu.VMEM((local, neighbors + 1, count, width), F32),
                pltpu.SMEM((local, total), jnp.int32),
                gathered,
            ]
            + [gathered] * (3 * ROUNDS)
            + [column] * (2 * ROUNDS)
            + [
                pltpu.SemaphoreType.DMA((2,)),
                pltpu.SemaphoreType.DMA((4 * ROUNDS + 2,)),
                pltpu.SemaphoreType.DMA((4 * ROUNDS + 2,)),
            ],
            compiler_params=pltpu.CompilerParams(
                collective_id=0, has_side_effects=True, vmem_limit_bytes=65408 * 1024
            ),
            name="solve_rounds",
        )(probes, factor, inverses, pattern.T, owner)
        sol, selected = pl.pallas_call(
            functools.partial(select_kernel, local, count, neighbors + 1),
            out_shape=(
                jax.ShapeDtypeStruct((local, count, width), BF16),
                jax.ShapeDtypeStruct((local, neighbors + 1, width, width), BF16),
            ),
            in_specs=[vmem, vmem],
            out_specs=(vmem, anywhere),
            scratch_shapes=[
                pltpu.VMEM((local, neighbors + 1, width, width), BF16),
                pltpu.SemaphoreType.DMA((local,)),
            ],
            compiler_params=pltpu.CompilerParams(vmem_limit_bytes=16 * 1024 * 1024),
            name="select_blocks",
        )(backed, near)
        return sol, selected

    return jax.shard_map(
        body,
        mesh=mesh,
        in_specs=(
            P("rows", "probes", None),
            P("rows", None, None, None),
            P("rows", None, None),
            P(),
            P(),
        ),
        out_specs=(P("rows", "probes", None), P("rows", "probes", None, None)),
        check_vma=False,
    )
```

time: 48.6 us -> 57.8 us (1.19)
  Pallas kernels: 47.7 us -> 55.4 us
  local copies, waits for them, and re-layouts: 0 us -> 1.47 us
    pallas_call x1, Pallas kernels: 44.8 us -> 53.3 us  [body(): pl.pallas_call(functools.partial(solve_kernel, n, inner, local, count, ne...]
    unnamed x0 -> x4, local copies, waits for them, and re-layouts: none -> 1.47 us
    pallas_call x1, Pallas kernels: 2.85 us -> 2.06 us  [body(): pl.pallas_call(functools.partial(select_kernel, local, count, neighbors +...]
where the time goes in v3:
time: 57.8 us; the launch traced here: 57.5 us
  Pallas kernels  55.4 us (96%)
  local copies, waits for them, and re-layouts  1.47 us (3%)
  between operations  0.65 us (1%)
    pallas_call x1, Pallas kernels, body(): pl.pallas_call(functools.partial(solve_kernel, n, inner, local, count, ne...  53.3 us
    pallas_call x1, Pallas kernels, body(): pl.pallas_call(functools.partial(select_kernel, local, count, neighbors +...  2.06 us
    unnamed x4, local copies, waits for them, and re-layouts  1.47 us

profile of v3, /device:TPU:0, one launch (start us, length us, event | category | flops | bytes accessed | tf_op | source)
XLA Modules:
  0.0 57.5 jit_solution(635518715086861153)
XLA Ops:
  0.6 53.3 %solve_rounds.1 = (bf16[2,8,256]{2,1,0:T(8,128)(2,1)}, bf16[2,8,1280]{2,1,0:T(8,128)(2,1)}) custom-call(bf16[2,8,256]{2,1,0:T(8,128)(2,1)} %refs_0_.1, bf16[2,4,256,256]{3,2,1,0:T(8,128)(2,1)} %refs_1_.1, bf16[2,256,256]{2,1,0:T(8,128)(2,1)} %refs_2_.1, s32[4,32]{1,0:T(4,128)} %bitcast.1, s32[32]{0:T(128)} %refs_4_.1), custom_call_target="tpu_custom_call" | custom-call | tf_op jit(solution)/shard_map/solve_rounds/pallas_call | solution.py:301
  54.0 0.0 copy-start
  54.0 0.8 %copy-done = bf16[2,8,1280]{2,1,0:T(8,128)(2,1)S(1)} copy-done((bf16[2,8,1280]{2,1,0:T(8,128)(2,1)S(1)}, bf16[2,8,1280]{2,1,0:T(8,128)(2,1)}, u32[]{:S(2)}) %copy-start) | copy-done | bytes 40984
  54.8 0.0 copy-start.1
  54.8 0.7 %copy-done.1 = bf16[2,8,256]{2,1,0:T(8,128)(2,1)S(1)} copy-done((bf16[2,8,256]{2,1,0:T(8,128)(2,1)S(1)}, bf16[2,8,256]{2,1,0:T(8,128)(2,1)}, u32[]{:S(2)}) %copy-start.1) | copy-done | bytes 8216
  55.5 2.1 %select_blocks.1 = (bf16[2,8,256]{2,1,0:T(8,128)(2,1)}, bf16[2,5,256,256]{3,2,1,0:T(8,128)(2,1)}) custom-call(bf16[2,8,256]{2,1,0:T(8,128)(2,1)S(1)} %copy-done.1, bf16[2,8,1280]{2,1,0:T(8,128)(2,1)S(1)} %copy-done), custom_call_target="tpu_custom_call" | custom-call | tf_op jit(solution)/shard_map/select_blocks/pallas_call | solution.py:330
Async XLA Ops:
  54.0 0.8 %copy-start = (bf16[2,8,1280]{2,1,0:T(8,128)(2,1)S(1)}, bf16[2,8,1280]{2,1,0:T(8,128)(2,1)}, u32[]{:S(2)}) copy-start(bf16[2,8,1280]{2,1,0:T(8,128)(2,1)} %get-tuple-element.5.near_ref) | copy-start | bytes 122884
  54.8 0.7 %copy-start.1 = (bf16[2,8,256]{2,1,0:T(8,128)(2,1)S(1)}, bf16[2,8,256]{2,1,0:T(8,128)(2,1)}, u32[]{:S(2)}) copy-start(bf16[2,8,256]{2,1,0:T(8,128)(2,1)} %get-tuple-element.4.back_ref) | copy-start | bytes 24580

commit v4 on v2

v4 whole, which is shorter than its diff:
```python
import functools

import jax
import jax.numpy as jnp
from jax import lax
from jax.experimental import pallas as pl
from jax.experimental.pallas import tpu as pltpu
from jax.sharding import PartitionSpec as P

LEVELS = 4
ROUNDS = LEVELS - 1
STREAMS = 2
MESH = pl.DeviceIdType.MESH
F32 = jnp.float32
BF16 = jnp.bfloat16


def dot_nt(a, b):
    return lax.dot_general(a, b, (((1,), (1,)), ((), ())), preferred_element_type=F32)


def dot_nn(a, b):
    return lax.dot_general(a, b, (((1,), (0,)), ((), ())), preferred_element_type=F32)


def dot_tn(a, b):
    return lax.dot_general(a, b, (((0,), (0,)), ((), ())), preferred_element_type=F32)


def solve_kernel(n, local, count, neighbors, total, *refs):
    probes_ref, factor_hbm, inv_hbm, pattern_ref, owner_ref = refs[:5]
    back_ref, near_ref = refs[5:7]
    scratch = refs[7:]
    factor_ref, inv_ref, factor_t, inv_t, table_ref, all_probes = scratch[:6]
    terms_refs = scratch[6 : 6 + STREAMS]
    buffers = scratch[6 + STREAMS : 6 + STREAMS * (1 + 3 * ROUNDS)]
    load_sem, send_sem, recv_sem = scratch[6 + STREAMS * (1 + 3 * ROUNDS) :]

    def buffer(kind, turn, s):
        return buffers[(kind * ROUNDS + turn) * STREAMS + s]

    unroll = n <= 16
    group = max(g for g in range(1, 6) if (n - 1) % g == 0)
    width = probes_ref.shape[2]
    half = width // 2
    few = count // STREAMS
    rows = local * few
    probes_at = 2 * ROUNDS * STREAMS
    me = lax.axis_index("rows")

    load_inv = pltpu.make_async_copy(inv_hbm, inv_ref, load_sem.at[0])
    load_factor = pltpu.make_async_copy(factor_hbm, factor_ref, load_sem.at[1])
    load_inv.start()
    load_factor.start()

    def peer(step):
        odd = step % 2
        away = n // 2 + odd * ((step + 1) // 2) - (1 - odd) * (step // 2)
        return lax.rem(me + away, n)

    barrier = pltpu.get_barrier_semaphore()

    def greet(step, carry):
        pl.semaphore_signal(barrier, inc=1, device_id={"rows": peer(step)}, device_id_type=MESH)
        return carry

    lax.fori_loop(0, n - 1, greet, 0, unroll=unroll)

    def fold(value):
        return jnp.concatenate([value[:, :half], value[:, half:]], axis=0).astype(BF16)

    def unfold(block):
        wide = block.astype(F32)
        return jnp.concatenate([wide[:rows], wide[rows:]], axis=1)

    own_row = lax.broadcasted_iota(jnp.int32, (rows, width), 0) // few

    def merge(values):
        result = values[0]
        for r in range(1, local):
            result = jnp.where(own_row == r, values[r], result)
        return result

    def turned(value, places):
        places = places % local
        if places == 0:
            return value
        cut = places * few
        return jnp.concatenate([value[cut:], value[:cut]], axis=0)

    def pick(block, at, r, valid):
        value = turned(block, local - r)
        for q in range(1, local):
            value = jnp.where(at == q, turned(block, q - r + local), value)
        return jnp.where(valid, value, jnp.zeros_like(value)).astype(BF16)

    def pick_probes(slot, valid):
        wide = all_probes[lax.div(slot, local)].astype(F32)
        at = lax.rem(slot, local)
        value = wide[:count]
        for r in range(1, local):
            value = jnp.where(at == r, wide[r * count : (r + 1) * count], value)
        return jnp.where(valid, value, jnp.zeros_like(value)).astype(BF16)

    def send(src, dst, to, at):
        return pltpu.make_async_remote_copy(
            src_ref=src,
            dst_ref=dst.at[me],
            send_sem=send_sem.at[at],
            recv_sem=recv_sem.at[at],
            device_id={"rows": to},
            device_id_type=MESH,
        )

    def whole_of(ref, at):
        every = ref.at[pl.ds(0, n - 1)]
        return pltpu.make_async_remote_copy(
            src_ref=every,
            dst_ref=every,
            send_sem=send_sem.at[at],
            recv_sem=recv_sem.at[at],
            device_id={"rows": peer(0)},
            device_id_type=MESH,
        )

    def broadcast(ref, at, first=0, last=n - 1):
        def one(step, carry):
            send(ref.at[me], ref, peer(step), at).start()
            return carry

        lax.fori_loop(first, last, one, 0, unroll=unroll)

    def share_probes(turn):
        pieces = 2 * ROUNDS - 1
        size = -(-(n - 1) // pieces)
        first = min(turn * size, n - 1)
        last = min(first + size, n - 1)
        if last > first:
            broadcast(all_probes, probes_at, first, last)

    whole = [probes_ref[r].astype(F32) for r in range(local)]
    all_probes[me] = jnp.concatenate(whole, axis=0).astype(BF16)
    probes = [
        jnp.concatenate([w[s * few : (s + 1) * few] for w in whole], axis=0)
        for s in range(STREAMS)
    ]

    load_inv.wait()
    solved = []
    for s in range(STREAMS):
        value = merge([dot_nt(probes[s].astype(BF16), inv_ref[r]) for r in range(local)])
        solved.append(value)
        buffer(0, 0, s)[me] = fold(value)

    pl.semaphore_wait(barrier, n - 1)
    for s in range(STREAMS):
        broadcast(buffer(0, 0, s), s)
    share_probes(0)

    sources, places, valids = [], [], []
    for r in range(local):
        slot = me * local + r
        row = lax.fori_loop(
            0, total, lambda i, found: jnp.where(owner_ref[i] == slot, i, found), 0, unroll=8
        )
        cols = [pattern_ref[k, row] for k in range(neighbors)]
        valids.append([c >= 0 for c in cols])
        slots = [owner_ref[jnp.maximum(c, 0)] for c in cols]
        sources.append(slots)
        places.append([(lax.div(s, local), lax.rem(s, local)) for s in slots])

    def fill(slot, carry):
        for r in range(local):
            found = neighbors
            for k in range(neighbors):
                here = jnp.logical_and(sources[r][k] == slot, valids[r][k])
                found = jnp.where(here, k, found)
            table_ref[r, slot] = found
        return carry

    lax.fori_loop(0, total, fill, 0, unroll=4)
    for s in range(STREAMS):
        for r in range(local):
            terms_refs[s][r, neighbors] = jnp.zeros((rows, width), F32)

    load_factor.wait()
    for r in range(local):
        inv_t[r] = inv_ref[r].T
        for k in range(neighbors):
            factor_t[r, k] = factor_ref[r, k].T

    def step_ahead(level, s):
        last = buffer(0, level - 1, s)
        whole_of(last, (level - 1) * STREAMS + s).wait_recv()
        sums = []
        for r in range(local):
            value = jnp.zeros((rows, width), F32)
            for k in range(neighbors):
                device, at = places[r][k]
                near = pick(unfold(last[device]), at, r, valids[r][k])
                value += dot_nn(near, factor_t[r, k])
            sums.append(value)
        resid = (probes[s] - merge(sums)).astype(BF16)
        solved[s] = merge([dot_nn(resid, inv_t[r]) for r in range(local)])
        if level < ROUNDS:
            ref = buffer(0, level, s)
            ref[me] = fold(solved[s])
            broadcast(ref, level * STREAMS + s)

    backed = [None] * STREAMS

    def step_back(turn, s):
        ended = solved[s].astype(BF16).astype(F32)
        if turn > 0:
            into = buffer(2, turn - 1, s)
            whole_of(into, (ROUNDS + turn - 1) * STREAMS + s).wait_recv()
            acc = into[0].astype(F32)
            for d in range(1, n):
                acc += into[d].astype(F32)
            ended = ended - jnp.concatenate([acc[:rows], acc[rows:]], axis=1)
        start = ended.astype(BF16)
        value = merge([dot_nn(start, inv_ref[r]) for r in range(local)]).astype(BF16)
        backed[s] = value
        if turn == ROUNDS:
            return
        terms_ref = terms_refs[s]
        for r in range(local):
            for k in range(neighbors):
                term = dot_nn(value, factor_ref[r, k])
                terms_ref[r, k] = merge([turned(term, r - q + local) for q in range(local)])

        def part(device):
            values = []
            for q in range(local):
                slot = device * local + q
                found = terms_ref[0, table_ref[0, slot]]
                for r in range(1, local):
                    found += terms_ref[r, table_ref[r, slot]]
                values.append(found)
            return fold(merge(values))

        out, into = buffer(1, turn, s), buffer(2, turn, s)
        at = (ROUNDS + turn) * STREAMS + s

        def some(chunk, carry):
            steps = [chunk * group + i for i in range(group)]
            parts = [part(peer(step)) for step in steps]
            for step, value in zip(steps, parts):
                out[peer(step)] = value
            for step in steps:
                send(out.at[peer(step)], into, peer(step), at).start()
            return carry

        lax.fori_loop(0, (n - 1) // group, some, 0, unroll=unroll)
        into[me] = part(me)

    for level in range(1, LEVELS):
        for s in range(STREAMS):
            step_ahead(level, s)
            if level == ROUNDS:
                step_back(0, s)
        share_probes(level)
    for turn in range(1, LEVELS):
        for s in range(STREAMS):
            step_back(turn, s)
        if turn < ROUNDS - 1:
            share_probes(ROUNDS + turn)

    whole_of(all_probes, probes_at).wait_recv()
    wide = [value.astype(F32) for value in backed]
    for r in range(local):
        back_ref[r] = jnp.concatenate(
            [value[r * few : (r + 1) * few] for value in wide], axis=0
        ).astype(BF16)
        for k in range(neighbors):
            near_ref[r, :, k * width : (k + 1) * width] = pick_probes(sources[r][k], valids[r][k])
        near_ref[r, :, neighbors * width :] = whole[r].astype(BF16)

    for turn in range(ROUNDS):
        for s in range(STREAMS):
            whole_of(buffer(0, turn, s), turn * STREAMS + s).wait_send()
            whole_of(buffer(1, turn, s), (ROUNDS + turn) * STREAMS + s).wait_send()
    whole_of(all_probes, probes_at).wait_send()


def select_kernel(local, count, blocks, back_ref, near_ref, sol_ref, sel_hbm, sel_ref, sems):
    copies = []
    width = back_ref.shape[2]
    for r in range(local):
        value = back_ref[r]
        sol_ref[r] = value
        near = near_ref[r]
        for k in range(blocks):
            product = dot_tn(value, near[:, k * width : (k + 1) * width])
            sel_ref[r, k] = (product / count).astype(BF16)
        copy = pltpu.make_async_copy(sel_ref.at[r], sel_hbm.at[r], sems.at[r])
        copy.start()
        copies.append(copy)
    for copy in copies:
        copy.wait()


def solution(mesh):
    n = mesh.shape["rows"]

    def body(probes, factor, inverses, pattern, owner):
        local, count, width = probes.shape
        neighbors = factor.shape[1]
        total = owner.shape[0]
        rows = local * count
        vmem = pl.BlockSpec(memory_space=pltpu.VMEM)
        smem = pl.BlockSpec(memory_space=pltpu.SMEM)
        anywhere = pl.BlockSpec(memory_space=pl.ANY)
        backed, near = pl.pallas_call(
            functools.partial(solve_kernel, n, local, count, neighbors, total),
            out_shape=(
                jax.ShapeDtypeStruct((local, count, width), BF16),
                jax.ShapeDtypeStruct((local, count, (neighbors + 1) * width), BF16),
            ),
            in_specs=[vmem, anywhere, anywhere, smem, smem],
            out_specs=(vmem, vmem),
            scratch_shapes=[
                pltpu.VMEM(factor.shape, BF16),
                pltpu.VMEM(inverses.shape, BF16),
                pltpu.VMEM(factor.shape, BF16),
                pltpu.VMEM(inverses.shape, BF16),
                pltpu.SMEM((local, total), jnp.int32),
                pltpu.VMEM((n, rows, width), BF16),
            ]
            + [pltpu.VMEM((local, neighbors + 1, rows // STREAMS, width), F32)] * STREAMS
            + [pltpu.VMEM((n, 2 * rows // STREAMS, width // 2), BF16)] * (3 * ROUNDS * STREAMS)
            + [
                pltpu.SemaphoreType.DMA((2,)),
                pltpu.SemaphoreType.DMA((2 * ROUNDS * STREAMS + 1,)),
                pltpu.SemaphoreType.DMA((2 * ROUNDS * STREAMS + 1,)),
            ],
            compiler_params=pltpu.CompilerParams(
                collective_id=0, has_side_effects=True, vmem_limit_bytes=60 * 1024 * 1024
            ),
            name="solve_rounds",
        )(probes, factor, inverses, pattern.T, owner)
        sol, selected = pl.pallas_call(
            functools.partial(select_kernel, local, count, neighbors + 1),
            out_shape=(
                jax.ShapeDtypeStruct((local, count, width), BF16),
                jax.ShapeDtypeStruct((local, neighbors + 1, width, width), BF16),
            ),
            in_specs=[vmem, vmem],
            out_specs=(vmem, anywhere),
            scratch_shapes=[
                pltpu.VMEM((local, neighbors + 1, width, width), BF16),
                pltpu.SemaphoreType.DMA((local,)),
            ],
            compiler_params=pltpu.CompilerParams(vmem_limit_bytes=60 * 1024 * 1024),
            name="select_blocks",
        )(backed, near)
        return sol, selected

    return jax.shard_map(
        body,
        mesh=mesh,
        in_specs=(
            P("rows", "probes", None),
            P("rows", None, None, None),
            P("rows", None, None),
            P(),
            P(),
        ),
        out_specs=(P("rows", "probes", None), P("rows", "probes", None, None)),
        check_vma=False,
    )
```

time: 48.6 us -> 46.2 us (0.951)
  Pallas kernels: 47.7 us -> 45.2 us
    pallas_call x1, Pallas kernels: 44.8 us -> 42.4 us  [body(): pl.pallas_call(functools.partial(solve_kernel, n, local, count, neighbors...]
where the time goes in v4:
time: 46.2 us; the launch traced here: 45.9 us
  Pallas kernels  45.2 us (98%)
  between operations  0.64 us (1%)
    pallas_call x1, Pallas kernels, body(): pl.pallas_call(functools.partial(solve_kernel, n, local, count, neighbors...  42.4 us
    pallas_call x1, Pallas kernels, body(): pl.pallas_call(functools.partial(select_kernel, local, count, neighbors +...  2.85 us

profile of v4, /device:TPU:0, one launch (start us, length us, event | category | flops | bytes accessed | tf_op | source)
XLA Modules:
  0.0 45.9 jit_solution(9597268154355518285)
XLA Ops:
  0.6 42.4 %solve_rounds.1 = (bf16[2,8,256]{2,1,0:T(8,128)(2,1)}, bf16[2,8,1280]{2,1,0:T(8,128)(2,1)}) custom-call(bf16[2,8,256]{2,1,0:T(8,128)(2,1)} %refs_0_.1, bf16[2,4,256,256]{3,2,1,0:T(8,128)(2,1)} %refs_1_.1, bf16[2,256,256]{2,1,0:T(8,128)(2,1)} %refs_2_.1, s32[4,32]{1,0:T(4,128)} %bitcast.1, s32[32]{0:T(128)} %refs_4_.1), custom_call_target="tpu_custom_call" | custom-call | tf_op jit(solution)/shard_map/solve_rounds/pallas_call | solution.py:314
  43.0 2.8 %select_blocks.1 = (bf16[2,8,256]{2,1,0:T(8,128)(2,1)}, bf16[2,5,256,256]{3,2,1,0:T(8,128)(2,1)}) custom-call(bf16[2,8,256]{2,1,0:T(8,128)(2,1)} %get-tuple-element.4.back_ref, bf16[2,8,1280]{2,1,0:T(8,128)(2,1)} %get-tuple-element.5.near_ref), custom_call_target="tpu_custom_call" | custom-call | tf_op jit(solution)/shard_map/select_blocks/pallas_call | solution.py:342

commit v5 on v4

--- a/solution.py
+++ b/solution.py
@@ -31,10 +31,10 @@
     probes_ref, factor_hbm, inv_hbm, pattern_ref, owner_ref = refs[:5]
     back_ref, near_ref = refs[5:7]
     scratch = refs[7:]
-    factor_ref, inv_ref, factor_t, inv_t, table_ref, all_probes = scratch[:6]
-    terms_refs = scratch[6 : 6 + STREAMS]
-    buffers = scratch[6 + STREAMS : 6 + STREAMS * (1 + 3 * ROUNDS)]
-    load_sem, send_sem, recv_sem = scratch[6 + STREAMS * (1 + 3 * ROUNDS) :]
+    factor_ref, inv_ref, factor_t, inv_t, table_ref, all_probes, lent, found_ref, taken = scratch[:9]
+    terms_refs = scratch[9 : 9 + STREAMS]
+    buffers = scratch[9 + STREAMS : 9 + STREAMS * (1 + 3 * ROUNDS)]
+    load_sem, send_sem, recv_sem = scratch[9 + STREAMS * (1 + 3 * ROUNDS) :]
 
     def buffer(kind, turn, s):
         return buffers[(kind * ROUNDS + turn) * STREAMS + s]
@@ -42,16 +42,23 @@
     unroll = n <= 16
     group = max(g for g in range(1, 6) if (n - 1) % g == 0)
     width = probes_ref.shape[2]
-    half = width // 2
-    few = count // STREAMS
+    few = count
     rows = local * few
     probes_at = 2 * ROUNDS * STREAMS
+    lend_at, return_at = probes_at + 1, probes_at + 2
     me = lax.axis_index("rows")
+    core = lax.axis_index("probes")
+    leads = core % 2 == 1
+    helps = core % 2 == 0
+    partner = core + 1 - 2 * (core % 2)
 
     load_inv = pltpu.make_async_copy(inv_hbm, inv_ref, load_sem.at[0])
     load_factor = pltpu.make_async_copy(factor_hbm, factor_ref, load_sem.at[1])
-    load_inv.start()
-    load_factor.start()
+
+    @pl.when(leads)
+    def _():
+        load_inv.start()
+        load_factor.start()
 
     def peer(step):
         odd = step % 2
@@ -65,13 +72,7 @@
         return carry
 
     lax.fori_loop(0, n - 1, greet, 0, unroll=unroll)
-
-    def fold(value):
-        return jnp.concatenate([value[:, :half], value[:, half:]], axis=0).astype(BF16)
-
-    def unfold(block):
-        wide = block.astype(F32)
-        return jnp.concatenate([wide[:rows], wide[rows:]], axis=1)
+    pl.semaphore_signal(barrier, inc=1, device_id={"probes": partner}, device_id_type=MESH)
 
     own_row = lax.broadcasted_iota(jnp.int32, (rows, width), 0) // few
 
@@ -138,24 +139,41 @@
         if last > first:
             broadcast(all_probes, probes_at, first, last)
 
+    def pass_on(src, dst, at):
+        return pltpu.make_async_remote_copy(
+            src_ref=src,
+            dst_ref=dst,
+            send_sem=send_sem.at[at],
+            recv_sem=recv_sem.at[at],
+            device_id={"probes": partner},
+            device_id_type=MESH,
+        )
+
+    lend = pass_on(all_probes.at[me], lent, lend_at)
+    give_back = pass_on(found_ref, taken, return_at)
     whole = [probes_ref[r].astype(F32) for r in range(local)]
-    all_probes[me] = jnp.concatenate(whole, axis=0).astype(BF16)
-    probes = [
-        jnp.concatenate([w[s * few : (s + 1) * few] for w in whole], axis=0)
-        for s in range(STREAMS)
-    ]
-
-    load_inv.wait()
-    solved = []
-    for s in range(STREAMS):
-        value = merge([dot_nt(probes[s].astype(BF16), inv_ref[r]) for r in range(local)])
-        solved.append(value)
-        buffer(0, 0, s)[me] = fold(value)
-
-    pl.semaphore_wait(barrier, n - 1)
-    for s in range(STREAMS):
-        broadcast(buffer(0, 0, s), s)
-    share_probes(0)
+    stacked = jnp.concatenate(whole, axis=0)
+    all_probes[me] = stacked.astype(BF16)
+
+    def begin(s, value):
+        ended = merge([dot_nt(value, inv_ref[r]) for r in range(local)])
+        buffer(0, 0, s)[me] = ended.astype(BF16)
+
+    @pl.when(leads)
+    def _():
+        load_inv.wait()
+        begin(0, stacked.astype(BF16))
+
+    pl.semaphore_wait(barrier, n)
+
+    @pl.when(helps)
+    def _():
+        lend.start()
+        broadcast(all_probes, probes_at)
+
+    @pl.when(leads)
+    def _():
+        broadcast(buffer(0, 0, 0), 0)
 
     sources, places, valids = [], [], []
     for r in range(local):
@@ -178,16 +196,8 @@
             table_ref[r, slot] = found
         return carry
 
-    lax.fori_loop(0, total, fill, 0, unroll=4)
-    for s in range(STREAMS):
-        for r in range(local):
-            terms_refs[s][r, neighbors] = jnp.zeros((rows, width), F32)
-
-    load_factor.wait()
-    for r in range(local):
-        inv_t[r] = inv_ref[r].T
-        for k in range(neighbors):
-            factor_t[r, k] = factor_ref[r, k].T
+    solved = [None] * STREAMS
+    backed = [None] * STREAMS
 
     def step_ahead(level, s):
         last = buffer(0, level - 1, s)
@@ -197,17 +207,15 @@
             value = jnp.zeros((rows, width), F32)
             for k in range(neighbors):
                 device, at = places[r][k]
-                near = pick(unfold(last[device]), at, r, valids[r][k])
+                near = pick(last[device].astype(F32), at, r, valids[r][k])
                 value += dot_nn(near, factor_t[r, k])
             sums.append(value)
-        resid = (probes[s] - merge(sums)).astype(BF16)
+        resid = ((lent if s else all_probes.at[me])[...].astype(F32) - merge(sums)).astype(BF16)
         solved[s] = merge([dot_nn(resid, inv_t[r]) for r in range(local)])
         if level < ROUNDS:
             ref = buffer(0, level, s)
-            ref[me] = fold(solved[s])
+            ref[me] = solved[s].astype(BF16)
             broadcast(ref, level * STREAMS + s)
-
-    backed = [None] * STREAMS
 
     def step_back(turn, s):
         ended = solved[s].astype(BF16).astype(F32)
@@ -217,7 +225,7 @@
             acc = into[0].astype(F32)
             for d in range(1, n):
                 acc += into[d].astype(F32)
-            ended = ended - jnp.concatenate([acc[:rows], acc[rows:]], axis=1)
+            ended = ended - acc
         start = ended.astype(BF16)
         value = merge([dot_nn(start, inv_ref[r]) for r in range(local)]).astype(BF16)
         backed[s] = value
@@ -237,7 +245,7 @@
                 for r in range(1, local):
                     found += terms_ref[r, table_ref[r, slot]]
                 values.append(found)
-            return fold(merge(values))
+            return merge(values).astype(BF16)
 
         out, into = buffer(1, turn, s), buffer(2, turn, s)
         at = (ROUNDS + turn) * STREAMS + s
@@ -254,32 +262,60 @@
         lax.fori_loop(0, (n - 1) // group, some, 0, unroll=unroll)
         into[me] = part(me)
 
-    for level in range(1, LEVELS):
+    @pl.when(leads)
+    def _():
+        lend.wait_recv()
+        begin(1, lent[...])
+        broadcast(buffer(0, 0, 1), 1)
+        share_probes(0)
+        lax.fori_loop(0, total, fill, 0, unroll=4)
         for s in range(STREAMS):
-            step_ahead(level, s)
-            if level == ROUNDS:
-                step_back(0, s)
-        share_probes(level)
-    for turn in range(1, LEVELS):
-        for s in range(STREAMS):
-            step_back(turn, s)
-        if turn < ROUNDS - 1:
-            share_probes(ROUNDS + turn)
+            for r in range(local):
+                terms_refs[s][r, neighbors] = jnp.zeros((rows, width), F32)
+        load_factor.wait()
+        for r in range(local):
+            inv_t[r] = inv_ref[r].T
+            for k in range(neighbors):
+                factor_t[r, k] = factor_ref[r, k].T
+        for level in range(1, LEVELS):
+            for s in range(STREAMS):
+                step_ahead(level, s)
+                if level == ROUNDS:
+                    step_back(0, s)
+            share_probes(level)
+        for turn in range(1, LEVELS):
+            for s in range(STREAMS):
+                step_back(turn, s)
+            if turn < ROUNDS - 1:
+                share_probes(ROUNDS + turn)
+        found_ref[...] = backed[1]
+        give_back.start()
+        value = backed[0].astype(F32)
+        for r in range(local):
+            back_ref[r] = value[r * few : (r + 1) * few].astype(BF16)
 
     whole_of(all_probes, probes_at).wait_recv()
-    wide = [value.astype(F32) for value in backed]
     for r in range(local):
-        back_ref[r] = jnp.concatenate(
-            [value[r * few : (r + 1) * few] for value in wide], axis=0
-        ).astype(BF16)
         for k in range(neighbors):
             near_ref[r, :, k * width : (k + 1) * width] = pick_probes(sources[r][k], valids[r][k])
         near_ref[r, :, neighbors * width :] = whole[r].astype(BF16)
 
-    for turn in range(ROUNDS):
-        for s in range(STREAMS):
-            whole_of(buffer(0, turn, s), turn * STREAMS + s).wait_send()
-            whole_of(buffer(1, turn, s), (ROUNDS + turn) * STREAMS + s).wait_send()
+    @pl.when(leads)
+    def _():
+        for turn in range(ROUNDS):
+            for s in range(STREAMS):
+                whole_of(buffer(0, turn, s), turn * STREAMS + s).wait_send()
+                whole_of(buffer(1, turn, s), (ROUNDS + turn) * STREAMS + s).wait_send()
+        give_back.wait_send()
+
+    @pl.when(helps)
+    def _():
+        give_back.wait_recv()
+        value = taken[...].astype(F32)
+        for r in range(local):
+            back_ref[r] = value[r * few : (r + 1) * few].astype(BF16)
+        lend.wait_send()
+
     whole_of(all_probes, probes_at).wait_send()
 
 
@@ -326,13 +362,16 @@
                 pltpu.VMEM(inverses.shape, BF16),
                 pltpu.SMEM((local, total), jnp.int32),
                 pltpu.VMEM((n, rows, width), BF16),
+                pltpu.VMEM((rows, width), BF16),
+                pltpu.VMEM((rows, width), BF16),
+                pltpu.VMEM((rows, width), BF16),
             ]
-            + [pltpu.VMEM((local, neighbors + 1, rows // STREAMS, width), F32)] * STREAMS
-            + [pltpu.VMEM((n, 2 * rows // STREAMS, width // 2), BF16)] * (3 * ROUNDS * STREAMS)
+            + [pltpu.VMEM((local, neighbors + 1, rows, width), F32)] * STREAMS
+            + [pltpu.VMEM((n, rows, width), BF16)] * (3 * ROUNDS * STREAMS)
             + [
                 pltpu.SemaphoreType.DMA((2,)),
-                pltpu.SemaphoreType.DMA((2 * ROUNDS * STREAMS + 1,)),
-                pltpu.SemaphoreType.DMA((2 * ROUNDS * STREAMS + 1,)),
+                pltpu.SemaphoreType.DMA((2 * ROUNDS * STREAMS + 3,)),
+                pltpu.SemaphoreType.DMA((2 * ROUNDS * STREAMS + 3,)),
             ],
             compiler_params=pltpu.CompilerParams(
                 collective_id=0, has_side_effects=True, vmem_limit_bytes=60 * 1024 * 1024

time: 46.2 us -> 44.9 us (0.972)
  Pallas kernels: 45.2 us -> 44 us
    pallas_call x1, Pallas kernels: 42.4 us -> 41.1 us  [body(): pl.pallas_call(functools.partial(solve_kernel, n, local, count, neighbors...]
where the time goes in v5:
time: 44.9 us; the launch traced here: 44.6 us
  Pallas kernels  44 us (98%)
  between operations  0.64 us (1%)
    pallas_call x1, Pallas kernels, body(): pl.pallas_call(functools.partial(solve_kernel, n, local, count, neighbors...  41.1 us
    pallas_call x1, Pallas kernels, body(): pl.pallas_call(functools.partial(select_kernel, local, count, neighbors +...  2.85 us

profile of v5, /device:TPU:0, one launch (start us, length us, event | category | flops | bytes accessed | tf_op | source)
XLA Modules:
  0.0 44.6 jit_solution(12523624317350337990)
XLA Ops:
  0.6 41.1 %solve_rounds.1 = (bf16[2,8,256]{2,1,0:T(8,128)(2,1)}, bf16[2,8,1280]{2,1,0:T(8,128)(2,1)}) custom-call(bf16[2,8,256]{2,1,0:T(8,128)(2,1)} %refs_0_.1, bf16[2,4,256,256]{3,2,1,0:T(8,128)(2,1)} %refs_1_.1, bf16[2,256,256]{2,1,0:T(8,128)(2,1)} %refs_2_.1, s32[4,32]{1,0:T(4,128)} %bitcast.1, s32[32]{0:T(128)} %refs_4_.1), custom_call_target="tpu_custom_call" | custom-call | tf_op jit(solution)/shard_map/solve_rounds/pallas_call | solution.py:350
  41.8 2.8 %select_blocks.1 = (bf16[2,8,256]{2,1,0:T(8,128)(2,1)}, bf16[2,5,256,256]{3,2,1,0:T(8,128)(2,1)}) custom-call(bf16[2,8,256]{2,1,0:T(8,128)(2,1)} %get-tuple-element.4.back_ref, bf16[2,8,1280]{2,1,0:T(8,128)(2,1)} %get-tuple-element.5.near_ref), custom_call_target="tpu_custom_call" | custom-call | tf_op jit(solution)/shard_map/select_blocks/pallas_call | solution.py:381

commit v6 on v5

--- a/solution.py
+++ b/solution.py
@@ -27,14 +27,16 @@
     return lax.dot_general(a, b, (((0,), (0,)), ((), ())), preferred_element_type=F32)
 
 
-def solve_kernel(n, local, count, neighbors, total, *refs):
-    probes_ref, factor_hbm, inv_hbm, pattern_ref, owner_ref = refs[:5]
+def solve_kernel(n, inner, local, count, neighbors, total, *refs):
+    probes_hbm, factor_hbm, inv_hbm, pattern_hbm, owner_hbm = refs[:5]
     back_ref, near_ref = refs[5:7]
     scratch = refs[7:]
-    factor_ref, inv_ref, factor_t, inv_t, table_ref, all_probes, lent, found_ref, taken = scratch[:9]
-    terms_refs = scratch[9 : 9 + STREAMS]
-    buffers = scratch[9 + STREAMS : 9 + STREAMS * (1 + 3 * ROUNDS)]
-    load_sem, send_sem, recv_sem = scratch[9 + STREAMS * (1 + 3 * ROUNDS) :]
+    factor_ref, inv_ref, factor_t, inv_t, table_ref, probes_ref, pattern_ref, owner_ref = scratch[:8]
+    pairs, own_probes, lent, found_ref, taken, near_out, near_in = scratch[8:15]
+    terms_refs = scratch[15 : 15 + STREAMS]
+    buffers = scratch[15 + STREAMS : 15 + STREAMS * (1 + 3 * ROUNDS)]
+    load_sem, send_sem, recv_sem = scratch[15 + STREAMS * (1 + 3 * ROUNDS) :]
+    outer = n // inner
 
     def buffer(kind, turn, s):
         return buffers[(kind * ROUNDS + turn) * STREAMS + s]
@@ -45,7 +47,7 @@
     few = count
     rows = local * few
     probes_at = 2 * ROUNDS * STREAMS
-    lend_at, return_at = probes_at + 1, probes_at + 2
+    lend_at, return_at, near_at = probes_at + 2, probes_at + 3, probes_at + 4
     me = lax.axis_index("rows")
     core = lax.axis_index("probes")
     leads = core % 2 == 1
@@ -54,10 +56,20 @@
 
     load_inv = pltpu.make_async_copy(inv_hbm, inv_ref, load_sem.at[0])
     load_factor = pltpu.make_async_copy(factor_hbm, factor_ref, load_sem.at[1])
+    load_probes = pltpu.make_async_copy(probes_hbm, probes_ref, load_sem.at[2])
+    load_pattern = pltpu.make_async_copy(pattern_hbm, pattern_ref, load_sem.at[3])
+    load_owner = pltpu.make_async_copy(owner_hbm, owner_ref, load_sem.at[4])
+    load_probes.start()
 
     @pl.when(leads)
     def _():
         load_inv.start()
+
+    load_pattern.start()
+    load_owner.start()
+
+    @pl.when(leads)
+    def _():
         load_factor.start()
 
     def peer(step):
@@ -95,12 +107,14 @@
             value = jnp.where(at == q, turned(block, q - r + local), value)
         return jnp.where(valid, value, jnp.zeros_like(value)).astype(BF16)
 
-    def pick_probes(slot, valid):
-        wide = all_probes[lax.div(slot, local)].astype(F32)
+    def pick_pair(slot, valid, first):
+        device = lax.div(slot, local)
+        block = pairs[lax.rem(device, inner), lax.div(device, inner)].astype(F32)
         at = lax.rem(slot, local)
-        value = wide[:count]
+        value = block[first : first + count]
         for r in range(1, local):
-            value = jnp.where(at == r, wide[r * count : (r + 1) * count], value)
+            low_row = first + r * count
+            value = jnp.where(at == r, block[low_row : low_row + count], value)
         return jnp.where(valid, value, jnp.zeros_like(value)).astype(BF16)
 
     def send(src, dst, to, at):
@@ -131,14 +145,6 @@
 
         lax.fori_loop(first, last, one, 0, unroll=unroll)
 
-    def share_probes(turn):
-        pieces = 2 * ROUNDS - 1
-        size = -(-(n - 1) // pieces)
-        first = min(turn * size, n - 1)
-        last = min(first + size, n - 1)
-        if last > first:
-            broadcast(all_probes, probes_at, first, last)
-
     def pass_on(src, dst, at):
         return pltpu.make_async_remote_copy(
             src_ref=src,
@@ -149,11 +155,13 @@
             device_id_type=MESH,
         )
 
-    lend = pass_on(all_probes.at[me], lent, lend_at)
+    lend = pass_on(own_probes, lent, lend_at)
     give_back = pass_on(found_ref, taken, return_at)
+    give_near = pass_on(near_out, near_in, near_at)
+    load_probes.wait()
     whole = [probes_ref[r].astype(F32) for r in range(local)]
     stacked = jnp.concatenate(whole, axis=0)
-    all_probes[me] = stacked.astype(BF16)
+    own_probes[...] = stacked.astype(BF16)
 
     def begin(s, value):
         ended = merge([dot_nt(value, inv_ref[r]) for r in range(local)])
@@ -166,14 +174,14 @@
 
     pl.semaphore_wait(barrier, n)
 
-    @pl.when(helps)
-    def _():
-        lend.start()
-        broadcast(all_probes, probes_at)
+    lend.start()
 
     @pl.when(leads)
     def _():
         broadcast(buffer(0, 0, 0), 0)
+
+    load_pattern.wait()
+    load_owner.wait()
 
     sources, places, valids = [], [], []
     for r in range(local):
@@ -210,7 +218,7 @@
                 near = pick(last[device].astype(F32), at, r, valids[r][k])
                 value += dot_nn(near, factor_t[r, k])
             sums.append(value)
-        resid = ((lent if s else all_probes.at[me])[...].astype(F32) - merge(sums)).astype(BF16)
+        resid = ((lent if s else own_probes)[...].astype(F32) - merge(sums)).astype(BF16)
         solved[s] = merge([dot_nn(resid, inv_t[r]) for r in range(local)])
         if level < ROUNDS:
             ref = buffer(0, level, s)
@@ -267,7 +275,6 @@
         lend.wait_recv()
         begin(1, lent[...])
         broadcast(buffer(0, 0, 1), 1)
-        share_probes(0)
         lax.fori_loop(0, total, fill, 0, unroll=4)
         for s in range(STREAMS):
             for r in range(local):
@@ -282,26 +289,19 @@
                 step_ahead(level, s)
                 if level == ROUNDS:
                     step_back(0, s)
-            share_probes(level)
         for turn in range(1, LEVELS):
             for s in range(STREAMS):
                 step_back(turn, s)
-            if turn < ROUNDS - 1:
-                share_probes(ROUNDS + turn)
         found_ref[...] = backed[1]
         give_back.start()
         value = backed[0].astype(F32)
         for r in range(local):
             back_ref[r] = value[r * few : (r + 1) * few].astype(BF16)
 
-    whole_of(all_probes, probes_at).wait_recv()
-    for r in range(local):
-        for k in range(neighbors):
-            near_ref[r, :, k * width : (k + 1) * width] = pick_probes(sources[r][k], valids[r][k])
-        near_ref[r, :, neighbors * width :] = whole[r].astype(BF16)
-
-    @pl.when(leads)
-    def _():
+        give_near.wait_recv()
+        handed = near_in[...].astype(F32)
+        for r in range(local):
+            near_ref[r, :, : neighbors * width] = handed[r * count : (r + 1) * count].astype(BF16)
         for turn in range(ROUNDS):
             for s in range(STREAMS):
                 whole_of(buffer(0, turn, s), turn * STREAMS + s).wait_send()
@@ -310,13 +310,59 @@
 
     @pl.when(helps)
     def _():
+        high, low = me // inner, me % inner
+        lend.wait_recv()
+        pairs[low, high] = jnp.concatenate([stacked, lent[...].astype(F32)], axis=0).astype(BF16)
+
+        def to_far(step, src):
+            to = lax.rem(high + step, outer) * inner + low
+            return pltpu.make_async_remote_copy(
+                src_ref=src,
+                dst_ref=src,
+                send_sem=send_sem.at[probes_at],
+                recv_sem=recv_sem.at[probes_at],
+                device_id={"rows": to},
+                device_id_type=MESH,
+            )
+
+        def to_near(step, src):
+            to = high * inner + lax.rem(low + step, inner)
+            return pltpu.make_async_remote_copy(
+                src_ref=src,
+                dst_ref=src,
+                send_sem=send_sem.at[probes_at + 1],
+                recv_sem=recv_sem.at[probes_at + 1],
+                device_id={"rows": to},
+                device_id_type=MESH,
+            )
+
+        for step in range(1, outer):
+            to_far(step, pairs.at[low, high]).start()
+        far_all = to_far(1, pairs.at[0, pl.ds(0, outer - 1)])
+        far_all.wait_recv()
+        for step in range(1, inner):
+            to_near(step, pairs.at[low]).start()
+        near_all = to_near(1, pairs.at[pl.ds(0, inner - 1)])
+        near_all.wait_recv()
+        for k in range(neighbors):
+            span = slice(k * width, (k + 1) * width)
+            theirs = []
+            for r in range(local):
+                near_ref[r, :, span] = pick_pair(sources[r][k], valids[r][k], 0)
+                theirs.append(pick_pair(sources[r][k], valids[r][k], rows).astype(F32))
+            near_out[:, span] = jnp.concatenate(theirs, axis=0).astype(BF16)
+        give_near.start()
+        far_all.wait_send()
+        near_all.wait_send()
         give_back.wait_recv()
         value = taken[...].astype(F32)
         for r in range(local):
             back_ref[r] = value[r * few : (r + 1) * few].astype(BF16)
-        lend.wait_send()
-
-    whole_of(all_probes, probes_at).wait_send()
+        give_near.wait_send()
+
+    for r in range(local):
+        near_ref[r, :, neighbors * width :] = whole[r].astype(BF16)
+    lend.wait_send()
 
 
 def select_kernel(local, count, blocks, back_ref, near_ref, sol_ref, sel_hbm, sel_ref, sems):
@@ -338,6 +384,7 @@
 
 def solution(mesh):
     n = mesh.shape["rows"]
+    inner = max(d for d in range(1, n + 1) if n % d == 0 and d * d <= n)
 
     def body(probes, factor, inverses, pattern, owner):
         local, count, width = probes.shape
@@ -345,15 +392,14 @@
         total = owner.shape[0]
         rows = local * count
         vmem = pl.BlockSpec(memory_space=pltpu.VMEM)
-        smem = pl.BlockSpec(memory_space=pltpu.SMEM)
         anywhere = pl.BlockSpec(memory_space=pl.ANY)
         backed, near = pl.pallas_call(
-            functools.partial(solve_kernel, n, local, count, neighbors, total),
+            functools.partial(solve_kernel, n, inner, local, count, neighbors, total),
             out_shape=(
                 jax.ShapeDtypeStruct((local, count, width), BF16),
                 jax.ShapeDtypeStruct((local, count, (neighbors + 1) * width), BF16),
             ),
-            in_specs=[vmem, anywhere, anywhere, smem, smem],
+            in_specs=[pl.BlockSpec(memory_space=pltpu.HBM)] * 5,
             out_specs=(vmem, vmem),
             scratch_shapes=[
                 pltpu.VMEM(factor.shape, BF16),
@@ -361,17 +407,19 @@
                 pltpu.VMEM(factor.shape, BF16),
                 pltpu.VMEM(inverses.shape, BF16),
                 pltpu.SMEM((local, total), jnp.int32),
-                pltpu.VMEM((n, rows, width), BF16),
-                pltpu.VMEM((rows, width), BF16),
-                pltpu.VMEM((rows, width), BF16),
-                pltpu.VMEM((rows, width), BF16),
+                pltpu.VMEM(probes.shape, BF16),
+                pltpu.SMEM((neighbors, total), jnp.int32),
+                pltpu.SMEM((total,), jnp.int32),
+                pltpu.VMEM((inner, n // inner, 2 * rows, width), BF16),
             ]
+            + [pltpu.VMEM((rows, width), BF16)] * 4
+            + [pltpu.VMEM((rows, neighbors * width), BF16)] * 2
             + [pltpu.VMEM((local, neighbors + 1, rows, width), F32)] * STREAMS
             + [pltpu.VMEM((n, rows, width), BF16)] * (3 * ROUNDS * STREAMS)
             + [
-                pltpu.SemaphoreType.DMA((2,)),
-                pltpu.SemaphoreType.DMA((2 * ROUNDS * STREAMS + 3,)),
-                pltpu.SemaphoreType.DMA((2 * ROUNDS * STREAMS + 3,)),
+                pltpu.SemaphoreType.DMA((5,)),
+                pltpu.SemaphoreType.DMA((2 * ROUNDS * STREAMS + 5,)),
+                pltpu.SemaphoreType.DMA((2 * ROUNDS * STREAMS + 5,)),
             ],
             compiler_params=pltpu.CompilerParams(
                 collective_id=0, has_side_effects=True, vmem_limit_bytes=60 * 1024 * 1024

time: 44.9 us -> 43.8 us (0.976)
  Pallas kernels: 44 us -> 42.8 us
    pallas_call x1, Pallas kernels: 41.1 us -> 40 us  [body(): pl.pallas_call(functools.partial(solve_kernel, n, inner, local, count, ne...]
where the time goes in v6:
time: 43.8 us; the launch traced here: 43.5 us
  Pallas kernels  42.8 us (98%)
  between operations  0.64 us (1%)
    pallas_call x1, Pallas kernels, body(): pl.pallas_call(functools.partial(solve_kernel, n, inner, local, count, ne...  40 us
    pallas_call x1, Pallas kernels, body(): pl.pallas_call(functools.partial(select_kernel, local, count, neighbors +...  2.85 us

profile of v6, /device:TPU:0, one launch (start us, length us, event | category | flops | bytes accessed | tf_op | source)
XLA Modules:
  0.0 43.5 jit_solution(13215608012442006092)
XLA Ops:
  0.6 40.0 %solve_rounds.1 = (bf16[2,8,256]{2,1,0:T(8,128)(2,1)}, bf16[2,8,1280]{2,1,0:T(8,128)(2,1)}) custom-call(bf16[2,8,256]{2,1,0:T(8,128)(2,1)} %refs_0_.1, bf16[2,4,256,256]{3,2,1,0:T(8,128)(2,1)} %refs_1_.1, bf16[2,256,256]{2,1,0:T(8,128)(2,1)} %refs_2_.1, s32[4,32]{1,0:T(4,128)} %bitcast.1, s32[32]{0:T(128)} %refs_4_.1), custom_call_target="tpu_custom_call" | custom-call | tf_op jit(solution)/shard_map/solve_rounds/pallas_call | solution.py:396
  40.6 2.8 %select_blocks.1 = (bf16[2,8,256]{2,1,0:T(8,128)(2,1)}, bf16[2,5,256,256]{3,2,1,0:T(8,128)(2,1)}) custom-call(bf16[2,8,256]{2,1,0:T(8,128)(2,1)} %get-tuple-element.4.back_ref, bf16[2,8,1280]{2,1,0:T(8,128)(2,1)} %get-tuple-element.5.near_ref), custom_call_target="tpu_custom_call" | custom-call | tf_op jit(solution)/shard_map/select_blocks/pallas_call | solution.py:429

commit v7 on v6

--- a/solution.py
+++ b/solution.py
@@ -31,11 +31,11 @@
     probes_hbm, factor_hbm, inv_hbm, pattern_hbm, owner_hbm = refs[:5]
     back_ref, near_ref = refs[5:7]
     scratch = refs[7:]
-    factor_ref, inv_ref, factor_t, inv_t, table_ref, probes_ref, pattern_ref, owner_ref = scratch[:8]
-    pairs, own_probes, lent, found_ref, taken, near_out, near_in = scratch[8:15]
-    terms_refs = scratch[15 : 15 + STREAMS]
-    buffers = scratch[15 + STREAMS : 15 + STREAMS * (1 + 3 * ROUNDS)]
-    load_sem, send_sem, recv_sem = scratch[15 + STREAMS * (1 + 3 * ROUNDS) :]
+    factor_ref, inv_ref, table_ref, probes_ref, pattern_ref, owner_ref = scratch[:6]
+    pairs, own_probes, lent, found_ref, taken, near_out, near_in = scratch[6:13]
+    terms_refs = scratch[13 : 13 + STREAMS]
+    buffers = scratch[13 + STREAMS : 13 + STREAMS * (1 + 3 * ROUNDS)]
+    load_sem, send_sem, recv_sem = scratch[13 + STREAMS * (1 + 3 * ROUNDS) :]
     outer = n // inner
 
     def buffer(kind, turn, s):
@@ -216,10 +216,10 @@
             for k in range(neighbors):
                 device, at = places[r][k]
                 near = pick(last[device].astype(F32), at, r, valids[r][k])
-                value += dot_nn(near, factor_t[r, k])
+                value += dot_nt(near, factor_ref[r, k])
             sums.append(value)
         resid = ((lent if s else own_probes)[...].astype(F32) - merge(sums)).astype(BF16)
-        solved[s] = merge([dot_nn(resid, inv_t[r]) for r in range(local)])
+        solved[s] = merge([dot_nt(resid, inv_ref[r]) for r in range(local)])
         if level < ROUNDS:
             ref = buffer(0, level, s)
             ref[me] = solved[s].astype(BF16)
@@ -249,11 +249,12 @@
             values = []
             for q in range(local):
                 slot = device * local + q
-                found = terms_ref[0, table_ref[0, slot]]
+                own = slice(q * few, (q + 1) * few)
+                found = terms_ref[0, table_ref[0, slot], own]
                 for r in range(1, local):
-                    found += terms_ref[r, table_ref[r, slot]]
+                    found += terms_ref[r, table_ref[r, slot], own]
                 values.append(found)
-            return merge(values).astype(BF16)
+            return jnp.concatenate(values, axis=0).astype(BF16)
 
         out, into = buffer(1, turn, s), buffer(2, turn, s)
         at = (ROUNDS + turn) * STREAMS + s
@@ -275,25 +276,24 @@
         lend.wait_recv()
         begin(1, lent[...])
         broadcast(buffer(0, 0, 1), 1)
-        lax.fori_loop(0, total, fill, 0, unroll=4)
-        for s in range(STREAMS):
-            for r in range(local):
-                terms_refs[s][r, neighbors] = jnp.zeros((rows, width), F32)
         load_factor.wait()
-        for r in range(local):
-            inv_t[r] = inv_ref[r].T
-            for k in range(neighbors):
-                factor_t[r, k] = factor_ref[r, k].T
         for level in range(1, LEVELS):
             for s in range(STREAMS):
                 step_ahead(level, s)
                 if level == ROUNDS:
                     step_back(0, s)
-        for turn in range(1, LEVELS):
+            if level == 1:
+                lax.fori_loop(0, total, fill, 0, unroll=4)
+                for s in range(STREAMS):
+                    for r in range(local):
+                        terms_refs[s][r, neighbors] = jnp.zeros((rows, width), F32)
+        for turn in range(1, ROUNDS):
             for s in range(STREAMS):
                 step_back(turn, s)
+        step_back(ROUNDS, 1)
         found_ref[...] = backed[1]
         give_back.start()
+        step_back(ROUNDS, 0)
         value = backed[0].astype(F32)
         for r in range(local):
             back_ref[r] = value[r * few : (r + 1) * few].astype(BF16)
@@ -402,8 +402,6 @@
             in_specs=[pl.BlockSpec(memory_space=pltpu.HBM)] * 5,
             out_specs=(vmem, vmem),
             scratch_shapes=[
-                pltpu.VMEM(factor.shape, BF16),
-                pltpu.VMEM(inverses.shape, BF16),
                 pltpu.VMEM(factor.shape, BF16),
                 pltpu.VMEM(inverses.shape, BF16),
                 pltpu.SMEM((local, total), jnp.int32),

time: 43.8 us -> 44.2 us (level)
  Pallas kernels: 42.8 us -> 43.3 us
    pallas_call x1, Pallas kernels: 40 us -> 40.4 us  [body(): pl.pallas_call(functools.partial(solve_kernel, n, inner, local, count, ne...]
where the time goes in v7:
time: 44.2 us; the launch traced here: 43.9 us
  Pallas kernels  43.3 us (98%)
  between operations  0.64 us (1%)
    pallas_call x1, Pallas kernels, body(): pl.pallas_call(functools.partial(solve_kernel, n, inner, local, count, ne...  40.4 us
    pallas_call x1, Pallas kernels, body(): pl.pallas_call(functools.partial(select_kernel, local, count, neighbors +...  2.85 us

profile of v7, /device:TPU:0, one launch (start us, length us, event | category | flops | bytes accessed | tf_op | source)
XLA Modules:
  0.0 43.9 jit_solution(708836319178008443)
XLA Ops:
  0.6 40.4 %solve_rounds.1 = (bf16[2,8,256]{2,1,0:T(8,128)(2,1)}, bf16[2,8,1280]{2,1,0:T(8,128)(2,1)}) custom-call(bf16[2,8,256]{2,1,0:T(8,128)(2,1)} %refs_0_.1, bf16[2,4,256,256]{3,2,1,0:T(8,128)(2,1)} %refs_1_.1, bf16[2,256,256]{2,1,0:T(8,128)(2,1)} %refs_2_.1, s32[4,32]{1,0:T(4,128)} %bitcast.1, s32[32]{0:T(128)} %refs_4_.1), custom_call_target="tpu_custom_call" | custom-call | tf_op jit(solution)/shard_map/solve_rounds/pallas_call | solution.py:396
  41.1 2.9 %select_blocks.1 = (bf16[2,8,256]{2,1,0:T(8,128)(2,1)}, bf16[2,5,256,256]{3,2,1,0:T(8,128)(2,1)}) custom-call(bf16[2,8,256]{2,1,0:T(8,128)(2,1)} %get-tuple-element.4.back_ref, bf16[2,8,1280]{2,1,0:T(8,128)(2,1)} %get-tuple-element.5.near_ref), custom_call_target="tpu_custom_call" | custom-call | tf_op jit(solution)/shard_map/select_blocks/pallas_call | solution.py:427

commit v8 on v7

--- a/solution.py
+++ b/solution.py
@@ -31,11 +31,11 @@
     probes_hbm, factor_hbm, inv_hbm, pattern_hbm, owner_hbm = refs[:5]
     back_ref, near_ref = refs[5:7]
     scratch = refs[7:]
-    factor_ref, inv_ref, table_ref, probes_ref, pattern_ref, owner_ref = scratch[:6]
-    pairs, own_probes, lent, found_ref, taken, near_out, near_in = scratch[6:13]
-    terms_refs = scratch[13 : 13 + STREAMS]
-    buffers = scratch[13 + STREAMS : 13 + STREAMS * (1 + 3 * ROUNDS)]
-    load_sem, send_sem, recv_sem = scratch[13 + STREAMS * (1 + 3 * ROUNDS) :]
+    factor_ref, inv_ref, factor_t, inv_t, table_ref, probes_ref, pattern_ref, owner_ref = scratch[:8]
+    pairs, own_probes, lent, found_ref, taken, near_out, near_in = scratch[8:15]
+    terms_refs = scratch[15 : 15 + STREAMS]
+    buffers = scratch[15 + STREAMS : 15 + STREAMS * (1 + 3 * ROUNDS)]
+    load_sem, send_sem, recv_sem = scratch[15 + STREAMS * (1 + 3 * ROUNDS) :]
     outer = n // inner
 
     def buffer(kind, turn, s):
@@ -212,14 +212,14 @@
         whole_of(last, (level - 1) * STREAMS + s).wait_recv()
         sums = []
         for r in range(local):
-            value = jnp.zeros((rows, width), F32)
+            near = []
             for k in range(neighbors):
                 device, at = places[r][k]
-                near = pick(last[device].astype(F32), at, r, valids[r][k])
-                value += dot_nt(near, factor_ref[r, k])
+                near.append(pick(last[device].astype(F32), at, r, valids[r][k]))
+            value = dot_nn(jnp.concatenate(near, axis=1), factor_t[r])
             sums.append(value)
         resid = ((lent if s else own_probes)[...].astype(F32) - merge(sums)).astype(BF16)
-        solved[s] = merge([dot_nt(resid, inv_ref[r]) for r in range(local)])
+        solved[s] = merge([dot_nn(resid, inv_t[r]) for r in range(local)])
         if level < ROUNDS:
             ref = buffer(0, level, s)
             ref[me] = solved[s].astype(BF16)
@@ -277,6 +277,10 @@
         begin(1, lent[...])
         broadcast(buffer(0, 0, 1), 1)
         load_factor.wait()
+        for r in range(local):
+            inv_t[r] = inv_ref[r].T
+            for k in range(neighbors):
+                factor_t[r, k * width : (k + 1) * width] = factor_ref[r, k].T
         for level in range(1, LEVELS):
             for s in range(STREAMS):
                 step_ahead(level, s)
@@ -403,6 +407,8 @@
             out_specs=(vmem, vmem),
             scratch_shapes=[
                 pltpu.VMEM(factor.shape, BF16),
+                pltpu.VMEM(inverses.shape, BF16),
+                pltpu.VMEM((local, neighbors * width, width), BF16),
                 pltpu.VMEM(inverses.shape, BF16),
                 pltpu.SMEM((local, total), jnp.int32),
                 pltpu.VMEM(probes.shape, BF16),

time: 44.2 us -> 43.7 us (0.989)
  Pallas kernels: 43.3 us -> 42.8 us
    pallas_call x1, Pallas kernels: 40.4 us -> 40 us  [body(): pl.pallas_call(functools.partial(solve_kernel, n, inner, local, count, ne...]
where the time goes in v8:
time: 43.7 us; the launch traced here: 43.4 us
  Pallas kernels  42.8 us (98%)
  between operations  0.64 us (1%)
    pallas_call x1, Pallas kernels, body(): pl.pallas_call(functools.partial(solve_kernel, n, inner, local, count, ne...  40 us
    pallas_call x1, Pallas kernels, body(): pl.pallas_call(functools.partial(select_kernel, local, count, neighbors +...  2.85 us

profile of v8, /device:TPU:0, one launch (start us, length us, event | category | flops | bytes accessed | tf_op | source)
XLA Modules:
  0.0 43.4 jit_solution(702997971482911649)
XLA Ops:
  0.6 40.0 %solve_rounds.1 = (bf16[2,8,256]{2,1,0:T(8,128)(2,1)}, bf16[2,8,1280]{2,1,0:T(8,128)(2,1)}) custom-call(bf16[2,8,256]{2,1,0:T(8,128)(2,1)} %refs_0_.1, bf16[2,4,256,256]{3,2,1,0:T(8,128)(2,1)} %refs_1_.1, bf16[2,256,256]{2,1,0:T(8,128)(2,1)} %refs_2_.1, s32[4,32]{1,0:T(4,128)} %bitcast.1, s32[32]{0:T(128)} %refs_4_.1), custom_call_target="tpu_custom_call" | custom-call | tf_op jit(solution)/shard_map/solve_rounds/pallas_call | solution.py:400
  40.6 2.8 %select_blocks.1 = (bf16[2,8,256]{2,1,0:T(8,128)(2,1)}, bf16[2,5,256,256]{3,2,1,0:T(8,128)(2,1)}) custom-call(bf16[2,8,256]{2,1,0:T(8,128)(2,1)} %get-tuple-element.4.back_ref, bf16[2,8,1280]{2,1,0:T(8,128)(2,1)} %get-tuple-element.5.near_ref), custom_call_target="tpu_custom_call" | custom-call | tf_op jit(solution)/shard_map/select_blocks/pallas_call | solution.py:433
